TPU v7x, 512 devices: a whole 4x4x16 slice. The times are simulated.
512 devices in a mesh: section: 32 (over y_lo, z), tensor: 16 (over y_hi, x, core).
Axes of the slice: x: 4, y: 4 (y_hi: 2, y_lo: 2; y = y_hi * 2 + y_lo), z: 16, core: 2. Of those that a mesh axis runs over, the one named last changes fastest.
Arguments:
- weight: bfloat16 [32, 2, 2560, 4096], P('section', None, None, 'tensor'), as said below
- stash_in: bfloat16 [32, 2, 2, 128, 2560], P('section', None, None, 'tensor'), may hold values from -6 to 6
- stash_pre: bfloat16 [32, 2, 2, 128, 4096], P('section', None, None, None, 'tensor'), may hold values from -6 to 6
- grad_in: bfloat16 [32, 2, 128, 2560], P('section', None, 'tensor'), may hold values from -1.5 to 1.5
- grad_loss: bfloat16 [2, 128, 2560], P(None, 'tensor'), may hold values from -1.5 to 1.5
Outputs:
- weight_grad: bfloat16 [32, 2560, 4096], P('section', None, 'tensor')
- grad_out: bfloat16 [32, 2, 128, 2560], P('section', None, 'tensor')
Inputs may be any that keep to these rules, and one draw needn't show every extreme that they name: weight[s, 1] equals weight[31 - s, 0] for every s: both copies of a section agree.
All inputs are finite; a program needn't handle non-finite values.
Results may differ from a plain program's by a relative error of at most 0.023.
Values may be sent and summed in bfloat16 or wider, within the bound.
No kernel may reach another device: no remote copies, remote signals or barrier semaphores. Data moves between devices by JAX's collectives and lax.ppermute only.
A program may use at most 64 MiB of HBM per device.

v0:
```python
import jax
import jax.numpy as jnp
from jax import lax
from jax.sharding import PartitionSpec as P

slope_c = 0.7978845608028654
cubic_c = 0.044715


def shifted(value, axis, steps):
    count = lax.axis_size(axis)
    first, last = (max(0, -steps), min(count, count - steps))
    return lax.ppermute(value, axis, [(source, source + steps) for source in range(first, last)])


def gelu_value(pre):
    inner = slope_c * (pre + cubic_c * pre * pre * pre)
    return 0.5 * pre * (1.0 + jnp.tanh(inner))


def gelu_slope(pre):
    inner = slope_c * (pre + cubic_c * pre * pre * pre)
    tanh_v = jnp.tanh(inner)
    return 0.5 * (1.0 + tanh_v) + 0.5 * pre * (1.0 - tanh_v * tanh_v) * slope_c * (
        1.0 + 3.0 * cubic_c * pre * pre
    )


def section_back(weight_k, inputs, pre, cotan):
    pre32 = pre.astype(jnp.float32)
    dhid = jnp.dot(cotan, weight_k, preferred_element_type=jnp.float32)
    dpre = (dhid * gelu_slope(pre32)).astype(jnp.bfloat16)
    hidden = gelu_value(pre32).astype(jnp.bfloat16)
    partial_value = lax.dot_general(
        dpre, weight_k, (((1,), (1,)), ((), ())), preferred_element_type=jnp.float32
    )
    wgrad = lax.dot_general(
        inputs, dpre, (((0,), (0,)), ((), ())), preferred_element_type=jnp.float32
    )
    wgrad = wgrad + lax.dot_general(
        cotan, hidden, (((0,), (0,)), ((), ())), preferred_element_type=jnp.float32
    )
    return (partial_value, wgrad)


def body(weight, stash_in, stash_pre, grad_in, grad_loss):
    sections = lax.axis_size("section")
    place = lax.axis_index("section")
    tensor_at = lax.axis_index("tensor")
    own = weight[0, 0]
    mirrored = weight[0, 1]
    depth = own.shape[0]
    width = own.shape[1]
    rows = grad_in.shape[2]
    cot_rows = grad_in[0]
    x_rows = stash_in[0].reshape(4, rows, depth)
    cot_full, loss_full, x_full = (
        lax.all_gather(cot_rows, "tensor", axis=1, tiled=True),
        lax.all_gather(grad_loss, "tensor", axis=1, tiled=True),
        lax.all_gather(x_rows, "tensor", axis=1, tiled=True),
    )
    tokens = cot_full.shape[1]
    x_full = x_full.reshape(2, 2, tokens, depth)
    pre = stash_pre[0]
    section_weights = (own, mirrored)
    cot_now = cot_full
    sums = [jnp.zeros((depth, width), jnp.float32), jnp.zeros((depth, width), jnp.float32)]
    result = None
    for tick in range(2):
        parts = []
        for pipe in range(2):
            part, wgrad = section_back(
                section_weights[pipe], x_full[pipe, tick], pre[pipe, tick], cot_now[pipe]
            )
            parts.append(part)
            sums[pipe] = sums[pipe] + wgrad
        partial_value = jnp.stack(parts)
        summed_dx = lax.psum(partial_value.astype(jnp.bfloat16), "tensor").astype(jnp.float32)
        new_dx = (summed_dx + cot_now.astype(jnp.float32)).astype(jnp.bfloat16)
        if tick == 0:
            down_in = shifted(new_dx[0], "section", -1)
            up_in = shifted(new_dx[1], "section", 1)
            arrived = jnp.stack([down_in, up_in])
        else:
            result = lax.dynamic_slice_in_dim(new_dx, tensor_at * rows, rows, 1)
        if tick == 0:
            down_cot = jnp.where(place == sections - 1, loss_full[0], arrived[0])
            up_cot = jnp.where(place == 0, loss_full[1], arrived[1])
            cot_now = jnp.stack([down_cot, up_cot])
    down_acc = sums[0].astype(jnp.bfloat16)
    up_acc = sums[1].astype(jnp.bfloat16)
    received = lax.all_to_all(
        jnp.stack([down_acc, up_acc]), "section", split_axis=1, concat_axis=0, tiled=True
    )
    received = received.reshape(sections, 2, depth // sections, width)
    paired = received[:, 0].astype(jnp.float32) + jnp.flip(received[:, 1], 0).astype(jnp.float32)
    final = lax.all_to_all(
        paired.astype(jnp.bfloat16), "section", split_axis=0, concat_axis=1, tiled=True
    )
    return (final, result[None])


def solution(mesh):
    return jax.shard_map(
        body,
        mesh=mesh,
        in_specs=(
            P("section", None, None, "tensor"),
            P("section", None, None, "tensor", None),
            P("section", None, None, None, "tensor"),
            P("section", None, "tensor", None),
            P(None, "tensor", None),
        ),
        out_specs=(P("section", None, "tensor"), P("section", None, "tensor", None)),
        check_vma=False,
    )
```

profile of v0, /device:TPU:1, one launch (start us, length us, event | category | flops | bytes accessed | tf_op | source)
XLA Modules:
  0.0 698.1 jit_solution(13662816461765957086)
XLA Ops:
  7.2 0.0 copy-start
  7.2 0.0 all-gather.9.cloned.1.call-start
  7.2 0.7 all-gather.9.cloned.1.call-update
  7.9 0.0 all-reduce.3.cloned.1.call-start
  8.0 70.5 %all-gather.9.cloned.1.call-done = bf16[1,2,128,2560]{3,2,1,0:T(8,128)(2,1)} async-done(((bf16[1,2,8,2560]{3,2,1,0:T(8,128)(2,1)}), bf16[1,2,128,2560]{3,2,1,0:T(8,128)(2,1)}) %all-gather.9.cloned.1.call-update) | async-done | bytes 1310736 | tf_op jit(solution)/shard_map/all_gather | solution.py:58
  78.4 1.9 fusion.41
  80.4 0.0 copy-done
  80.4 0.0 copy-start.9
  80.4 0.6 fusion.9
  81.0 0.0 copy-done.5
  81.0 0.0 copy-done.8
  81.0 0.3 fusion.47
  81.4 0.0 copy-done.9
  81.4 0.6 copy-done.10
  82.0 0.6 fusion.8
  82.6 1.2 pad_maximum_fusion.1
  83.7 0.0 all-reduce.3.cloned.1.call-update
  83.7 0.0 all-gather.7.cloned.1.call-start
  83.8 0.7 all-gather.7.cloned.1.call-update
  84.5 0.0 all-gather.5.cloned.1.call-start
  84.5 0.5 all-gather.5.cloned.1.call-update
  85.1 153.9 %all-reduce.3.cloned.1.call-done = bf16[2,128,2560]{2,1,0:T(8,128)(2,1)} async-done(((bf16[2,128,2560]{2,1,0:T(8,128)(2,1)}), bf16[2,128,2560]{2,1,0:T(8,128)(2,1)}) %all-reduce.3.cloned.1.call-update) | async-done | bytes 1310736 | tf_op jit(solution)/shard_map/psum | solution.py:78
  239.0 2.0 fusion.13
  241.0 0.9 slice_bitcast_fusion.10
  241.9 1.3 collective-permute-start
  243.2 4.8 collective-permute-start.1
  248.1 57.4 %all-gather.7.cloned.1.call-done = bf16[2,128,2560]{2,1,0:T(8,128)(2,1)} async-done(((bf16[2,8,2560]{2,1,0:T(8,128)(2,1)}), bf16[2,128,2560]{2,1,0:T(8,128)(2,1)}) %all-gather.7.cloned.1.call-update) | async-done | bytes 1310736 | tf_op jit(solution)/shard_map/all_gather | solution.py:59
  305.4 0.0 collective-permute-done
  305.4 0.0 collective-permute-done.1
  305.4 1.6 fusion.60
  307.1 0.8 copy-done.2
  307.9 1.0 fusion.38
  308.9 1.0 fusion.44
  309.9 63.5 %all-gather.5.cloned.1.call-done = bf16[4,128,2560]{2,1,0:T(8,128)(2,1)} async-done(((bf16[4,8,2560]{2,1,0:T(8,128)(2,1)}), bf16[4,128,2560]{2,1,0:T(8,128)(2,1)}) %all-gather.5.cloned.1.call-update) | async-done | bytes 2621456 | tf_op jit(solution)/shard_map/all_gather | solution.py:60
  373.4 1.8 fusion.59
  375.2 0.2 copy-done.7
  375.4 1.4 fusion.61
  376.7 0.0 copy-done.11
  376.8 0.0 copy-start.6
  376.8 0.5 convolution_bitcast_fusion
  377.3 0.5 convolution_bitcast_fusion.1
  377.8 0.2 copy-done.6
  378.1 0.5 fusion.3
  378.6 0.5 copy-done.3
  379.2 0.6 fusion.6
  379.7 0.5 fusion.2
  380.3 0.6 fusion.7
  380.8 0.2 pad_maximum_fusion
  381.1 4.7 copy.15
  385.8 132.3 %all_to_all.27 = bf16[2,2560,256]{2,0,1:T(2,128)(2,1)S(1)} all-to-all(bf16[2,2560,256]{2,0,1:T(2,128)(2,1)} %copy.15), channel_id=1, replica_groups=mesh['section'=32,'tensor'=16] {'section'}, dimensions={1} | all-to-all | bytes 5242880 | tf_op jit(solution)/shard_map/all_to_all | solution.py:92
  518.0 0.3 copy.16
  518.4 0.1 slice_bitcast_fusion
  518.5 0.0 copy-start.1
  518.5 1.4 fusion.12
  519.9 6.5 all-to-all-start.1
  526.4 0.0 all-reduce.5.cloned.1.call-start
  526.5 0.6 fusion.11
  527.1 0.6 fusion.10
  527.6 1.2 pad_maximum_fusion.2
  528.8 0.0 all-reduce.5.cloned.1.call-update
  528.9 158.7 %all-reduce.5.cloned.1.call-done = bf16[2,128,2560]{2,1,0:T(8,128)(2,1)} async-done(((bf16[2,128,2560]{2,1,0:T(8,128)(2,1)}), bf16[2,128,2560]{2,1,0:T(8,128)(2,1)}) %all-reduce.5.cloned.1.call-update) | async-done | bytes 1310736 | tf_op jit(solution)/shard_map/psum | solution.py:78
  687.6 1.5 fusion.119
  689.1 0.0 all-to-all-done.1
  689.1 2.5 copy.22
  (16 shorter events, 0.0 us)
Async XLA Ops:
  7.2 73.2 %copy-start = (bf16[1,2,2560,256]{3,2,1,0:T(8,128)(2,1)S(1)}, bf16[1,2,2560,256]{3,2,1,0:T(8,128)(2,1)}, u32[]{:S(2)}) copy-start(bf16[1,2,2560,256]{3,2,1,0:T(8,128)(2,1)} %param.5) | copy-start | bytes 7864324
  7.2 71.3 %all-gather.9.cloned.1.call-start = ((), (), s32[]{:S(2)}) async-start(), calls=%async_computation.6 | async-start | bytes 1392640 | tf_op jit(solution)/shard_map/all_gather | solution.py:58
  7.9 231.1 %all-reduce.3.cloned.1.call-start = ((), (), s32[]{:S(2)}) async-start(), calls=%async_computation.4 | async-start | bytes 2621440 | tf_op jit(solution)/shard_map/psum | solution.py:78
  78.4 2.5 copy-start.5
  78.4 2.6 copy-start.8
  80.4 1.0 copy-start.9
  81.4 0.6 copy-start.10
  83.7 221.7 %all-gather.7.cloned.1.call-start = ((), (), s32[]{:S(2)}) async-start(), calls=%async_computation.3 | async-start | bytes 1392640 | tf_op jit(solution)/shard_map/all_gather | solution.py:59
  84.5 288.9 %all-gather.5.cloned.1.call-start = ((), (), s32[]{:S(2)}) async-start(), calls=%async_computation.2 | async-start | bytes 2785280 | tf_op jit(solution)/shard_map/all_gather | solution.py:60
  241.9 63.5 %collective-permute-start = (bf16[128,2560]{1,0:T(8,128)(2,1)}, bf16[128,2560]{1,0:T(8,128)(2,1)}, u32[]{:S(2)}, u32[]{:S(2)}) collective-permute-start(bf16[128,2560]{1,0:T(8,128)(2,1)} %get-tuple-element.4), channel_id=1, source_target_pairs={{16,0},{32,16},{48,32},{64,48},{80,64},{96,80},{112,96},{128,112},... | collective-permute-start | bytes 1966088 | tf_op jit(solution)/shard_map/ppermute | solution.py:13
  243.2 62.2 %collective-permute-start.1 = (bf16[128,2560]{1,0:T(8,128)(2,1)S(1)}, bf16[128,2560]{1,0:T(8,128)(2,1)}, u32[]{:S(2)}, u32[]{:S(2)}) collective-permute-start(bf16[128,2560]{1,0:T(8,128)(2,1)S(1)} %get-tuple-element.5), channel_id=1, source_target_pairs={{0,16},{16,32},{32,48},{48,64},{64,80},{80,96},{96,112},{112,128},... | collective-permute-start | bytes 1966088 | tf_op jit(solution)/shard_map/ppermute | solution.py:13
  307.1 0.8 copy-start.2
  373.4 2.0 copy-start.7
  373.4 3.4 copy-start.11
  375.4 1.9 copy-start.13
  376.8 1.3 copy-start.6
  378.1 1.1 copy-start.3
  518.5 8.0 %copy-start.1 = (bf16[1,2,2560,256]{3,2,1,0:T(8,128)(2,1)S(1)}, bf16[1,2,2560,256]{3,2,1,0:T(8,128)(2,1)}, u32[]{:S(2)}) copy-start(bf16[1,2,2560,256]{3,2,1,0:T(8,128)(2,1)} %param.5) | copy-start | bytes 7864324
  518.5 8.0 %copy-start.12 = (bf16[128,256]{1,0:T(8,128)(2,1)S(1)}, bf16[128,256]{1,0:T(8,128)(2,1)}, u32[]{:S(2)}) copy-start(bf16[128,256]{1,0:T(8,128)(2,1)} %fusion.38) | copy-start | bytes 196612
  519.9 7.1 %copy-start.14 = (bf16[128,256]{1,0:T(8,128)(2,1)S(1)}, bf16[128,256]{1,0:T(8,128)(2,1)}, u32[]{:S(2)}) copy-start(bf16[128,256]{1,0:T(8,128)(2,1)} %fusion.44) | copy-start | bytes 196612
  519.9 169.2 %all-to-all-start.1 = ((bf16[32,80,256]{2,1,0:T(8,128)(2,1)}), bf16[32,80,256]{2,1,0:T(8,128)(2,1)}, u32[]{:S(2)}, u32[]{:S(2)}) async-start(bf16[32,80,256]{2,1,0:T(8,128)(2,1)} %fusion.12), calls=%async_computation.1 | async-start | bytes 2621440 | tf_op jit(solution)/shard_map/all_to_all | solution.py:97
  526.4 161.1 %all-reduce.5.cloned.1.call-start = ((), (), s32[]{:S(2)}) async-start(), calls=%async_computation.5 | async-start | bytes 2621440 | tf_op jit(solution)/shard_map/psum | solution.py:78
  527.6 159.9 %copy-start.4 = (bf16[128,2560]{1,0:T(8,128)(2,1)S(1)}, bf16[128,2560]{1,0:T(8,128)(2,1)}, u32[]{:S(2)}) copy-start(bf16[128,2560]{1,0:T(8,128)(2,1)} %copy-done.2) | copy-start | bytes 1966084
Sparse Core Ops, SparseCore 0:
  11.4 67.0 all-gather.8
  83.9 155.0 all-reduce.2
  242.3 63.0 all-gather.6
  308.6 64.6 all-gather.4
  529.9 157.6 all-reduce.4
where the time goes:
time: 699 us; the launch traced here: 698 us
  waiting for transfers between devices  506 us (72%)
  blocking collectives  132 us (19%)
  between operations  14.1 us (2%)
  matrix products  12.9 us (2%)
  starting transfers between devices  12.8 us (2%)
  local copies, waits for them, and re-layouts  10.9 us (2%)
  other arithmetic  9.23 us (1%)
    psum x2, waiting for transfers between devices, body(): lax.psum(partial_value.astype(jnp.bfloat16), 'tensor').astype(jnp.float32)  313 us
    all_to_all x1, blocking collectives, body(): lax.all_to_all(jnp.stack([down_acc, up_acc]), 'section', split_axis=1, co...  132 us
    all_gather x1, waiting for transfers between devices, body(): lax.all_gather(cot_rows, 'tensor', axis=1, tiled=True)  70.5 us
    all_gather x1, waiting for transfers between devices, body(): lax.all_gather(x_rows, 'tensor', axis=1, tiled=True)  63.5 us
    all_gather x1, waiting for transfers between devices, body(): lax.all_gather(grad_loss, 'tensor', axis=1, tiled=True)  57.4 us
  transfers between devices with their start and end apart: 8, of which 5 were waited for; matrix products, arithmetic and copies ran while one was open for 1% of the time, Pallas kernels for 0%

commit v1 on v0

v1 whole, which is shorter than its diff:
```python
import jax
import jax.numpy as jnp
from jax import lax
from jax.sharding import PartitionSpec as P

slope_c = 0.7978845608028654
cubic_c = 0.044715


def gelu_both(pre):
    inner = slope_c * (pre + cubic_c * pre * pre * pre)
    tanh_v = jnp.tanh(inner)
    value = 0.5 * pre * (1.0 + tanh_v)
    slope = 0.5 * (1.0 + tanh_v) + 0.5 * pre * (1.0 - tanh_v * tanh_v) * slope_c * (
        1.0 + 3.0 * cubic_c * pre * pre
    )
    return value, slope


def dot(a, b, over):
    return lax.dot_general(a, b, ((over[:1], over[1:]), ((), ())), preferred_element_type=jnp.float32)


def body(weight, stash_in, stash_pre, grad_in, grad_loss):
    sections = lax.axis_size("section")
    tensors = lax.axis_size("tensor")
    place = lax.axis_index("section")
    core = lax.axis_index("tensor") % 2
    bf16 = jnp.bfloat16
    mirror = [(s, sections - 1 - s) for s in range(sections)]
    swap = [(t, t ^ 1) for t in range(tensors)]
    pairs = ("section", "tensor")

    def flat(s, t):
        return s * tensors + t

    g_far = lax.ppermute(grad_in[0, 1], "section", mirror)
    own_w = weight[0, 0]
    other_w = lax.ppermute(own_w, "tensor", swap)
    pre_a = lax.ppermute(
        stash_pre[0, 1], pairs,
        [(flat(s, t), flat(sections - 1 - s, t)) for s in range(sections) for t in range(1, tensors, 2)],
    )
    pre_b = lax.ppermute(
        jnp.where(core == 0, stash_pre[0, 1], stash_pre[0, 0]), pairs,
        [(flat(s, t), flat(sections - 1 - s, t + 1)) for s in range(sections) for t in range(0, tensors, 2)]
        + [(flat(s, t), flat(s, t - 1)) for s in range(sections) for t in range(1, tensors, 2)],
    )
    x_far = lax.ppermute(stash_in[0, 1], "section", mirror)
    pre_own = jnp.where(core == 0, stash_pre[0, 0], pre_a)

    def to_cores(rows):
        blocks = jnp.broadcast_to(rows[None], (tensors // 2,) + rows.shape)
        blocks = blocks.reshape((tensors,) + rows.shape[1:])
        return lax.all_to_all(blocks, "tensor", 0, 0, tiled=True)

    def sum_rows(part):
        n = part.shape[0] // tensors
        blocks = lax.all_to_all(part.reshape(tensors, n, -1), "tensor", 0, 0, tiled=True)
        blocks = blocks.reshape(tensors // 2, 2, n, -1).astype(jnp.float32)
        return jnp.sum(blocks, axis=0)

    g_rows = jnp.stack([grad_in[0, 0], g_far])
    x_rows = jnp.stack([stash_in[0, 0], x_far])
    cots, dzs, hids = [], [], []
    dx_rows = None
    for tick in range(2):
        cot = to_cores(g_rows)
        cot = cot.reshape(-1, cot.shape[-1])
        h_a, slope_a = gelu_both(pre_own[tick].astype(jnp.float32))
        h_b, slope_b = gelu_both(pre_b[tick].astype(jnp.float32))
        dz_a = (dot(cot, own_w, (1, 0)) * slope_a).astype(bf16)
        dz_b = (dot(cot, other_w, (1, 0)) * slope_b).astype(bf16)
        part = dot(dz_a, own_w, (1, 1)) + dot(dz_b, other_w, (1, 1))
        dx_rows = (sum_rows(part.astype(bf16)) + g_rows.astype(jnp.float32)).astype(bf16)
        cots.append(cot)
        dzs.append((dz_a, dz_b))
        hids.append((h_a.astype(bf16), h_b.astype(bf16)))
        if tick == 0:
            down = lax.ppermute(dx_rows, "section", [(s, s - 1) for s in range(1, sections)])
            g_rows = jnp.where(place == sections - 1, grad_loss, down)
    back = lax.ppermute(dx_rows[1], "section", mirror)
    grad_out = jnp.stack([dx_rows[0], back])[None]

    x_all = to_cores(x_rows)
    x_all = x_all.reshape(-1, x_all.shape[-1])

    def as_x(first, second):
        return jnp.stack([v.reshape(tensors, -1, v.shape[-1]) for v in (first, second)], 1).reshape(
            -1, first.shape[-1]
        )

    left = jnp.concatenate([x_all] + cots, axis=0)
    accs = []
    for side in range(2):
        right = jnp.concatenate(
            [as_x(dzs[0][side], dzs[1][side]), hids[0][side], hids[1][side]], axis=0
        )
        accs.append(dot(left, right, (0, 0)).astype(bf16))
    theirs = lax.ppermute(accs[1], "tensor", swap)
    total = (accs[0].astype(jnp.float32) + theirs.astype(jnp.float32)).astype(bf16)
    return total[None], grad_out


def solution(mesh):
    return jax.shard_map(
        body,
        mesh=mesh,
        in_specs=(
            P("section", None, None, "tensor"),
            P("section", None, None, "tensor", None),
            P("section", None, None, None, "tensor"),
            P("section", None, "tensor", None),
            P(None, "tensor", None),
        ),
        out_specs=(P("section", None, "tensor"), P("section", None, "tensor", None)),
        check_vma=False,
    )
```

time: 699 us -> 174 us (0.25)
  the two profiles are of different devices: /device:TPU:1 before, /device:TPU:96 now
where the time goes in v1:
time: 174 us; the launch traced here: 172 us
  starting transfers between devices  77.2 us (44%)
  waiting for transfers between devices  40.8 us (23%)
  blocking collectives  23.5 us (14%)
  matrix products  18.9 us (11%)
  local copies, waits for them, and re-layouts  7.64 us (4%)
  other arithmetic  3.39 us (2%)
    all_to_all x1, blocking collectives, sum_rows(): lax.all_to_all(part.reshape(tensors, n, -1), 'tensor', 0, 0, tiled=True)  23.5 us
    ppermute x1, starting transfers between devices, body(): lax.ppermute(jnp.where(core == 0, stash_pre[0, 1], stash_pre[0, 0]), pair...  21.2 us
    dot_general x10, matrix products, dot(): lax.dot_general(a, b, ((over[:1], over[1:]), ((), ())), preferred_element...  18.9 us
    all_to_all x3, starting transfers between devices, to_cores(): return lax.all_to_all(blocks, 'tensor', 0, 0, tiled=True)  18.4 us
    all_to_all x3, waiting for transfers between devices, to_cores(): return lax.all_to_all(blocks, 'tensor', 0, 0, tiled=True)  12.9 us
    ppermute x1, starting transfers between devices, body(): g_far = lax.ppermute(grad_in[0, 1], 'section', mirror)  12.4 us
    all_to_all x1, waiting for transfers between devices, sum_rows(): lax.all_to_all(part.reshape(tensors, n, -1), 'tensor', 0, 0, tiled=True)  7.76 us
    ppermute x1, waiting for transfers between devices, body(): x_far = lax.ppermute(stash_in[0, 1], 'section', mirror)  7.04 us
  transfers between devices with their start and end apart: 12, of which 6 were waited for; matrix products, arithmetic and copies ran while one was open for 11% of the time, Pallas kernels for 0%

profile of v1, /device:TPU:96, one launch (start us, length us, event | category | flops | bytes accessed | tf_op | source)
XLA Modules:
  0.0 172.4 jit_solution(14359355113543969454)
XLA Ops:
  0.6 0.8 slice_bitcast_fusion.10
  1.4 12.4 %collective-permute-start.1 = (bf16[8,2560]{1,0:T(8,128)(2,1)S(1)}, bf16[8,2560]{1,0:T(8,128)(2,1)S(1)}, u32[]{:S(2)}, u32[]{:S(2)}) collective-permute-start(bf16[8,2560]{1,0:T(8,128)(2,1)S(1)} %get-tuple-element.13), channel_id=1, source_target_pairs={{0,496},{16,480},{32,464},{48,448},{64,432},{80,416},{96,400},{112... | collective-permute-start | bytes 122888 | tf_op jit(solution)/shard_map/ppermute | solution.py:37
  13.8 2.5 %slice_bitcast_fusion = bf16[2560,256]{1,0:T(8,128)(2,1)} fusion(bf16[1,2,2560,256]{3,2,1,0:T(8,128)(2,1)} %param.5), kind=kLoop, calls=%fused_computation.14 | loop fusion | bytes 2621440 | tf_op jit(solution)/shard_map/squeeze | solution.py:38
  16.3 2.0 %collective-permute-start.3 = (bf16[2560,256]{1,0:T(8,128)(2,1)}, bf16[2560,256]{1,0:T(8,128)(2,1)}, u32[]{:S(2)}, u32[]{:S(2)}) collective-permute-start(bf16[2560,256]{1,0:T(8,128)(2,1)} %slice_bitcast_fusion), channel_id=1, source_target_pairs={{0,1},{1,0},{2,3},{3,2},{4,5},{5,4},{6,7},{7,6},{8,9},{9,8},{10,11... | collective-permute-start | bytes 3932168 | tf_op jit(solution)/shard_map/ppermute | solution.py:39
  18.3 0.0 collective-permute-done.1
  18.3 0.0 copy-start.11
  18.4 0.0 copy-done.3
  18.4 0.0 copy-start
  18.4 0.9 broadcast_in_dim.11
  19.3 0.0 copy-done.11
  19.3 7.0 %all-to-all-start.1 = ((bf16[16,8,2560]{2,1,0:T(8,128)(2,1)}), bf16[16,8,2560]{2,1,0:T(8,128)(2,1)S(1)}, u32[]{:S(2)}, u32[]{:S(2)}) async-start(bf16[16,8,2560]{2,1,0:T(8,128)(2,1)} %bitcast.8), calls=%async_computation.1 | async-start | bytes 1310720 | tf_op jit(solution)/shard_map/all_to_all | solution.py:55
  26.3 0.0 copy-done.1
  26.3 0.7 slice_bitcast_fusion.1
  26.9 1.3 collective-permute-start.2
  28.2 0.0 collective-permute-done.2
  28.2 0.7 bitcast_select_fusion
  29.0 21.2 %collective-permute-start.4 = (bf16[2,128,256]{2,1,0:T(8,128)(2,1)}, bf16[2,128,256]{2,1,0:T(8,128)(2,1)S(1)}, u32[]{:S(2)}, u32[]{:S(2)}) collective-permute-start(bf16[2,128,256]{2,1,0:T(8,128)(2,1)} %get-tuple-element.2), channel_id=1, source_target_pairs={{0,497},{2,499},{4,501},{6,503},{8,505},{10,507},{12,509},{14,511}... | collective-permute-start | bytes 393224 | tf_op jit(solution)/shard_map/ppermute | solution.py:44
  50.2 0.0 all-to-all-done.1
  50.2 0.0 copy-done
  50.2 1.2 fusion.6
  51.4 0.0 copy-start.7
  51.4 0.6 fusion.63
  52.0 0.1 copy-done.7
  52.1 1.0 collective-permute-done.4
  53.0 0.0 collective-permute-done.3
  53.0 1.7 fusion.7
  54.8 0.0 copy-start.5
  54.8 1.9 %fusion.4 = bf16[16,8,2560]{2,1,0:T(8,128)(2,1)S(1)} fusion(f32[128,2560]{1,0:T(8,128)S(1)} %fusion.63, bf16[128,256]{1,0:T(8,128)(2,1)S(1)} %fusion.7, bf16[2560,256]{1,0:T(8,128)(2,1)} %collective-permute-done.3), kind=kOutput, calls=%fused_computation.8 | convolution fusion | flops 168427520 | bytes 3342336 | tf_op jit(solution)/shard_map/dot_general | solution.py:21
  56.7 0.0 copy-done.14
  56.7 0.0 copy-done.5
  56.7 0.0 copy-start.4
  56.7 23.5 %all_to_all.25 = bf16[16,8,2560]{2,1,0:T(8,128)(2,1)S(1)} all-to-all(bf16[16,8,2560]{2,1,0:T(8,128)(2,1)S(1)} %fusion.4), channel_id=1, replica_groups=mesh['section'=32,'tensor'=16] {'tensor'}, dimensions={0} | all-to-all | bytes 1310720 | tf_op jit(solution)/shard_map/all_to_all | solution.py:59
  80.2 0.1 convert_reduce_fusion.1
  80.3 0.0 copy-start.13
  80.3 2.1 %collective-permute-start.5 = (bf16[2,8,2560]{2,1,0:T(8,128)(2,1)S(1)}, bf16[2,8,2560]{2,1,0:T(8,128)(2,1)}, u32[]{:S(2)}, u32[]{:S(2)}) collective-permute-start(bf16[2,8,2560]{2,1,0:T(8,128)(2,1)S(1)} %add_convert_fusion.2), channel_id=1, source_target_pairs={{16,0},{32,16},{48,32},{64,48},{80,64},{96,80},{112,96},{128,112},... | collective-permute-start | bytes 245768 | tf_op jit(solution)/shard_map/ppermute | solution.py:80
  82.4 5.7 %collective-permute-done.5 = bf16[2,8,2560]{2,1,0:T(8,128)(2,1)} collective-permute-done((bf16[2,8,2560]{2,1,0:T(8,128)(2,1)S(1)}, bf16[2,8,2560]{2,1,0:T(8,128)(2,1)}, u32[]{:S(2)}, u32[]{:S(2)}) %collective-permute-start.5) | collective-permute-done | bytes 81952 | tf_op jit(solution)/shard_map/ppermute | solution.py:80
  88.1 0.9 broadcast_select_fusion
  89.0 0.9 broadcast_in_dim.12
  89.9 4.3 %all-to-all-start.3 = ((bf16[16,8,2560]{2,1,0:T(8,128)(2,1)}), bf16[16,8,2560]{2,1,0:T(8,128)(2,1)}, u32[]{:S(2)}, u32[]{:S(2)}) async-start(bf16[16,8,2560]{2,1,0:T(8,128)(2,1)} %bitcast.19), calls=%async_computation.3 | async-start | bytes 1310720 | tf_op jit(solution)/shard_map/all_to_all | solution.py:55
  94.2 6.9 %collective-permute-start = (bf16[2,8,2560]{2,1,0:T(8,128)(2,1)S(1)}, bf16[2,8,2560]{2,1,0:T(8,128)(2,1)S(1)}, u32[]{:S(2)}, u32[]{:S(2)}) collective-permute-start(bf16[2,8,2560]{2,1,0:T(8,128)(2,1)S(1)} %get-tuple-element.5), channel_id=1, source_target_pairs={{0,496},{16,480},{32,464},{48,448},{64,432},{80,416},{96,400},{112... | collective-permute-start | bytes 245768 | tf_op jit(solution)/shard_map/ppermute | solution.py:49
  101.1 7.0 %collective-permute-done = bf16[2,8,2560]{2,1,0:T(8,128)(2,1)S(1)} collective-permute-done((bf16[2,8,2560]{2,1,0:T(8,128)(2,1)S(1)}, bf16[2,8,2560]{2,1,0:T(8,128)(2,1)S(1)}, u32[]{:S(2)}, u32[]{:S(2)}) %collective-permute-start) | collective-permute-done | bytes 81952 | tf_op jit(solution)/shard_map/ppermute | solution.py:49
  108.2 0.0 all-to-all-done.3
  108.2 1.2 broadcast_in_dim.10
  109.4 7.2 %all-to-all-start = ((bf16[16,2,8,2560]{3,2,1,0:T(8,128)(2,1)}), bf16[16,2,8,2560]{3,2,1,0:T(8,128)(2,1)}, u32[]{:S(2)}, u32[]{:S(2)}) async-start(bf16[16,2,8,2560]{3,2,1,0:T(8,128)(2,1)} %bitcast.102), calls=%async_computation | async-start | bytes 2621440 | tf_op jit(solution)/shard_map/all_to_all | solution.py:55
  116.6 0.8 fusion.43
  117.4 1.8 %fusion.9 = bf16[128,256]{1,0:T(8,128)(2,1)S(1)} fusion(bf16[2560,256]{1,0:T(8,128)(2,1)} %collective-permute-done.3, bf16[2,128,256]{2,1,0:T(8,128)(2,1)} %copy-done.14, bf16[16,8,2560]{2,1,0:T(8,128)(2,1)} %all-to-all-done.3), kind=kOutput, calls=%fused_computation.22 | convolution fusion | flops 168427520 | bytes 2097152 | tf_op jit(solution)/shard_map/dot_general | solution.py:21
  119.2 1.4 fusion.8
  120.6 0.6 copy-done.9
  121.3 0.6 fusion.62
  121.8 2.7 %fusion.3 = bf16[16,8,2560]{2,1,0:T(8,128)(2,1)} fusion(f32[128,2560]{1,0:T(8,128)S(1)} %fusion.62, bf16[128,256]{1,0:T(8,128)(2,1)S(1)} %fusion.9, bf16[2560,256]{1,0:T(8,128)(2,1)} %collective-permute-done.3), kind=kOutput, calls=%fused_computation.7 | convolution fusion | flops 168427520 | bytes 3342336 | tf_op jit(solution)/shard_map/dot_general | solution.py:21
  124.6 12.9 %all-to-all-done = bf16[16,2,8,2560]{3,2,1,0:T(8,128)(2,1)} async-done(((bf16[16,2,8,2560]{3,2,1,0:T(8,128)(2,1)}), bf16[16,2,8,2560]{3,2,1,0:T(8,128)(2,1)}, u32[]{:S(2)}, u32[]{:S(2)}) %all-to-all-start) | async-done | bytes 1310752 | tf_op jit(solution)/shard_map/all_to_all | solution.py:55
  137.4 3.6 %all-to-all-start.4 = ((bf16[16,8,2560]{2,1,0:T(8,128)(2,1)}), bf16[16,8,2560]{2,1,0:T(8,128)(2,1)S(1)}, u32[]{:S(2)}, u32[]{:S(2)}) async-start(bf16[16,8,2560]{2,1,0:T(8,128)(2,1)} %fusion.3), calls=%async_computation.4 | async-start | bytes 1310720 | tf_op jit(solution)/shard_map/all_to_all | solution.py:59
  141.0 0.0 copy-done.15
  141.1 0.1 fusion.39
  141.2 3.5 %convolution_convert_fusion = bf16[2560,256]{1,0:T(8,128)(2,1)} fusion(bf16[128,2560]{1,0:T(8,128)(2,1)} %bitcast.20, bf16[128,2560]{1,0:T(8,128)(2,1)S(1)} %bitcast.105, bf16[256,2560]{1,0:T(8,128)(2,1)} %bitcast.4, bf16[128,256]{1,0:T(8,128)(2,1)S(1)} %get-tuple-element.9, bf16[128,256]{1,0:T(8,128)(2,1)S(1)} %get-tuple-element.8, ...), kind=kOutput, calls=%fused_computation | convolution fusion | flops 680394752 | bytes 4194304 | tf_op jit(solution)/shard_map/dot_general | solution.py:21
  144.7 2.3 %collective-permute-start.6 = (bf16[2560,256]{1,0:T(8,128)(2,1)}, bf16[2560,256]{1,0:T(8,128)(2,1)S(1)}, u32[]{:S(2)}, u32[]{:S(2)}) collective-permute-start(bf16[2560,256]{1,0:T(8,128)(2,1)} %convolution_convert_fusion), channel_id=1, source_target_pairs={{0,1},{1,0},{2,3},{3,2},{4,5},{5,4},{6,7},{7,6},{8,9},{9,8},{10,11... | collective-permute-start | bytes 3932168 | tf_op jit(solution)/shard_map/ppermute | solution.py:100
  147.0 7.8 %all-to-all-done.4 = bf16[16,8,2560]{2,1,0:T(8,128)(2,1)S(1)} async-done(((bf16[16,8,2560]{2,1,0:T(8,128)(2,1)}), bf16[16,8,2560]{2,1,0:T(8,128)(2,1)S(1)}, u32[]{:S(2)}, u32[]{:S(2)}) %all-to-all-start.4) | async-done | bytes 655392 | tf_op jit(solution)/shard_map/all_to_all | solution.py:59
  154.8 0.1 convert_reduce_fusion
  154.9 6.9 %collective-permute-start.7 = (bf16[8,2560]{1,0:T(8,128)(2,1)S(1)}, bf16[8,2560]{1,0:T(8,128)(2,1)S(1)}, u32[]{:S(2)}, u32[]{:S(2)}) collective-permute-start(bf16[8,2560]{1,0:T(8,128)(2,1)S(1)} %get-tuple-element.11), channel_id=1, source_target_pairs={{0,496},{16,480},{32,464},{48,448},{64,432},{80,416},{96,400},{112... | collective-permute-start | bytes 122888 | tf_op jit(solution)/shard_map/ppermute | solution.py:82
  161.9 6.4 %collective-permute-done.7 = bf16[8,2560]{1,0:T(8,128)(2,1)S(1)} collective-permute-done((bf16[8,2560]{1,0:T(8,128)(2,1)S(1)}, bf16[8,2560]{1,0:T(8,128)(2,1)S(1)}, u32[]{:S(2)}, u32[]{:S(2)}) %collective-permute-start.7) | collective-permute-done | bytes 40992 | tf_op jit(solution)/shard_map/ppermute | solution.py:82
  168.3 0.6 maximum_bitcast_fusion
  169.0 0.0 collective-permute-done.6
  169.0 0.0 copy-done.16
  169.0 3.5 %fusion.5 = bf16[1,2560,256]{2,1,0:T(8,128)(2,1)} fusion(bf16[2560,256]{1,0:T(8,128)(2,1)S(1)} %collective-permute-done.6, bf16[128,2560]{1,0:T(8,128)(2,1)} %bitcast.20, bf16[128,2560]{1,0:T(8,128)(2,1)S(1)} %bitcast.106, bf16[256,2560]{1,0:T(8,128)(2,1)} %bitcast.4, bf16[128,256]{1,0:T(8,128)(2,1)S(1)} %copy-done.17, bf16[128,256]{1,0:T(8,128)(2,1)S(1)} %copy-done.16, ...), kind=kOutput, calls=%fused_computation.11 | convolution fusion | flops 683016192 | bytes 5505024 | tf_op jit(solution)/shard_map/dot_general | solution.py:21
  (28 shorter events, 0.2 us)
Async XLA Ops:
  1.4 16.9 %copy-start.3 = (bf16[1,8,2560]{2,1,0:T(8,128)(2,1)}, bf16[1,8,2560]{2,1,0:T(8,128)(2,1)S(1)}, u32[]{:S(2)}) copy-start(bf16[1,8,2560]{2,1,0:T(8,128)(2,1)S(1)} %get-tuple-element.12) | copy-start | bytes 122884
  1.4 16.9 %collective-permute-start.1 = (bf16[8,2560]{1,0:T(8,128)(2,1)S(1)}, bf16[8,2560]{1,0:T(8,128)(2,1)S(1)}, u32[]{:S(2)}, u32[]{:S(2)}) collective-permute-start(bf16[8,2560]{1,0:T(8,128)(2,1)S(1)} %get-tuple-element.13), channel_id=1, source_target_pairs={{0,496},{16,480},{32,464},{48,448},{64,432},{80,416},{96,400},{112... | collective-permute-start | bytes 122888 | tf_op jit(solution)/shard_map/ppermute | solution.py:37
  16.3 10.0 %copy-start.1 = (bf16[1,2,2,128,256]{4,3,2,1,0:T(8,128)(2,1)S(1)}, bf16[1,2,2,128,256]{4,3,2,1,0:T(8,128)(2,1)}, u32[]{:S(2)}) copy-start(bf16[1,2,2,128,256]{4,3,2,1,0:T(8,128)(2,1)} %param.7) | copy-start | bytes 786436
  16.3 36.8 %collective-permute-start.3 = (bf16[2560,256]{1,0:T(8,128)(2,1)}, bf16[2560,256]{1,0:T(8,128)(2,1)}, u32[]{:S(2)}, u32[]{:S(2)}) collective-permute-start(bf16[2560,256]{1,0:T(8,128)(2,1)} %slice_bitcast_fusion), channel_id=1, source_target_pairs={{0,1},{1,0},{2,3},{3,2},{4,5},{5,4},{6,7},{7,6},{8,9},{9,8},{10,11... | collective-permute-start | bytes 3932168 | tf_op jit(solution)/shard_map/ppermute | solution.py:39
  18.3 0.9 copy-start.11
  18.4 31.8 %copy-start = (bf16[1,2,2560,256]{3,2,1,0:T(8,128)(2,1)S(1)}, bf16[1,2,2560,256]{3,2,1,0:T(8,128)(2,1)}, u32[]{:S(2)}) copy-start(bf16[1,2,2560,256]{3,2,1,0:T(8,128)(2,1)} %param.5) | copy-start | bytes 7864324
  19.3 30.9 %all-to-all-start.1 = ((bf16[16,8,2560]{2,1,0:T(8,128)(2,1)}), bf16[16,8,2560]{2,1,0:T(8,128)(2,1)S(1)}, u32[]{:S(2)}, u32[]{:S(2)}) async-start(bf16[16,8,2560]{2,1,0:T(8,128)(2,1)} %bitcast.8), calls=%async_computation.1 | async-start | bytes 1310720 | tf_op jit(solution)/shard_map/all_to_all | solution.py:55
  26.9 1.3 collective-permute-start.2
  29.0 24.1 %collective-permute-start.4 = (bf16[2,128,256]{2,1,0:T(8,128)(2,1)}, bf16[2,128,256]{2,1,0:T(8,128)(2,1)S(1)}, u32[]{:S(2)}, u32[]{:S(2)}) collective-permute-start(bf16[2,128,256]{2,1,0:T(8,128)(2,1)} %get-tuple-element.2), channel_id=1, source_target_pairs={{0,497},{2,499},{4,501},{6,503},{8,505},{10,507},{12,509},{14,511}... | collective-permute-start | bytes 393224 | tf_op jit(solution)/shard_map/ppermute | solution.py:44
  51.4 0.6 copy-start.7
  53.0 3.6 %copy-start.14 = (bf16[2,128,256]{2,1,0:T(8,128)(2,1)}, bf16[2,128,256]{2,1,0:T(8,128)(2,1)S(1)}, u32[]{:S(2)}) copy-start(bf16[2,128,256]{2,1,0:T(8,128)(2,1)S(1)} %collective-permute-done.4) | copy-start | bytes 393220
  54.8 1.9 %copy-start.5 = (bf16[128,256]{1,0:T(8,128)(2,1)}, bf16[128,256]{1,0:T(8,128)(2,1)S(1)}, u32[]{:S(2)}) copy-start(bf16[128,256]{1,0:T(8,128)(2,1)S(1)} %fusion.7) | copy-start | bytes 196612
  56.7 23.6 %copy-start.4 = (bf16[1,8,2560]{2,1,0:T(8,128)(2,1)S(1)}, bf16[1,8,2560]{2,1,0:T(8,128)(2,1)}, u32[]{:S(2)}) copy-start(bf16[1,8,2560]{2,1,0:T(8,128)(2,1)} %copy-done.3) | copy-start | bytes 122884
  56.7 23.6 %copy-start.12 = (bf16[8,2560]{1,0:T(8,128)(2,1)S(1)}, bf16[8,2560]{1,0:T(8,128)(2,1)}, u32[]{:S(2)}) copy-start(bf16[8,2560]{1,0:T(8,128)(2,1)} %copy-done.11) | copy-start | bytes 122884
  80.3 13.9 %copy-start.13 = (bf16[1,2,2,8,2560]{4,3,2,1,0:T(8,128)(2,1)S(1)}, bf16[1,2,2,8,2560]{4,3,2,1,0:T(8,128)(2,1)}, u32[]{:S(2)}) copy-start(bf16[1,2,2,8,2560]{4,3,2,1,0:T(8,128)(2,1)} %param.6) | copy-start | bytes 491524
  80.3 7.8 %collective-permute-start.5 = (bf16[2,8,2560]{2,1,0:T(8,128)(2,1)S(1)}, bf16[2,8,2560]{2,1,0:T(8,128)(2,1)}, u32[]{:S(2)}, u32[]{:S(2)}) collective-permute-start(bf16[2,8,2560]{2,1,0:T(8,128)(2,1)S(1)} %add_convert_fusion.2), channel_id=1, source_target_pairs={{16,0},{32,16},{48,32},{64,48},{80,64},{96,80},{112,96},{128,112},... | collective-permute-start | bytes 245768 | tf_op jit(solution)/shard_map/ppermute | solution.py:80
  89.9 18.3 %all-to-all-start.3 = ((bf16[16,8,2560]{2,1,0:T(8,128)(2,1)}), bf16[16,8,2560]{2,1,0:T(8,128)(2,1)}, u32[]{:S(2)}, u32[]{:S(2)}) async-start(bf16[16,8,2560]{2,1,0:T(8,128)(2,1)} %bitcast.19), calls=%async_computation.3 | async-start | bytes 1310720 | tf_op jit(solution)/shard_map/all_to_all | solution.py:55
  94.2 14.0 %collective-permute-start = (bf16[2,8,2560]{2,1,0:T(8,128)(2,1)S(1)}, bf16[2,8,2560]{2,1,0:T(8,128)(2,1)S(1)}, u32[]{:S(2)}, u32[]{:S(2)}) collective-permute-start(bf16[2,8,2560]{2,1,0:T(8,128)(2,1)S(1)} %get-tuple-element.5), channel_id=1, source_target_pairs={{0,496},{16,480},{32,464},{48,448},{64,432},{80,416},{96,400},{112... | collective-permute-start | bytes 245768 | tf_op jit(solution)/shard_map/ppermute | solution.py:49
  109.4 7.2 %copy-start.2 = (bf16[2,128,256]{2,1,0:T(8,128)(2,1)S(1)}, bf16[2,128,256]{2,1,0:T(8,128)(2,1)}, u32[]{:S(2)}) copy-start(bf16[2,128,256]{2,1,0:T(8,128)(2,1)} %get-tuple-element.3) | copy-start | bytes 393220
  109.4 28.1 %all-to-all-start = ((bf16[16,2,8,2560]{3,2,1,0:T(8,128)(2,1)}), bf16[16,2,8,2560]{3,2,1,0:T(8,128)(2,1)}, u32[]{:S(2)}, u32[]{:S(2)}) async-start(bf16[16,2,8,2560]{3,2,1,0:T(8,128)(2,1)} %bitcast.102), calls=%async_computation | async-start | bytes 2621440 | tf_op jit(solution)/shard_map/all_to_all | solution.py:55
  120.6 0.6 copy-start.9
  124.6 16.5 %copy-start.15 = (bf16[2,128,256]{2,1,0:T(8,128)(2,1)S(1)}, bf16[2,128,256]{2,1,0:T(8,128)(2,1)}, u32[]{:S(2)}) copy-start(bf16[2,128,256]{2,1,0:T(8,128)(2,1)} %copy-done.14) | copy-start | bytes 393220
  124.6 16.6 %copy-start.6 = (bf16[128,256]{1,0:T(8,128)(2,1)S(1)}, bf16[128,256]{1,0:T(8,128)(2,1)}, u32[]{:S(2)}) copy-start(bf16[128,256]{1,0:T(8,128)(2,1)} %copy-done.5) | copy-start | bytes 196612
  137.4 17.3 %all-to-all-start.4 = ((bf16[16,8,2560]{2,1,0:T(8,128)(2,1)}), bf16[16,8,2560]{2,1,0:T(8,128)(2,1)S(1)}, u32[]{:S(2)}, u32[]{:S(2)}) async-start(bf16[16,8,2560]{2,1,0:T(8,128)(2,1)} %fusion.3), calls=%async_computation.4 | async-start | bytes 1310720 | tf_op jit(solution)/shard_map/all_to_all | solution.py:59
  144.7 17.2 %copy-start.8 = (bf16[128,256]{1,0:T(8,128)(2,1)S(1)}, bf16[128,256]{1,0:T(8,128)(2,1)}, u32[]{:S(2)}) copy-start(bf16[128,256]{1,0:T(8,128)(2,1)} %copy-done.7) | copy-start | bytes 196612
  144.7 17.2 %copy-start.10 = (bf16[128,256]{1,0:T(8,128)(2,1)S(1)}, bf16[128,256]{1,0:T(8,128)(2,1)}, u32[]{:S(2)}) copy-start(bf16[128,256]{1,0:T(8,128)(2,1)} %copy-done.9) | copy-start | bytes 196612
  144.7 24.3 %copy-start.16 = (bf16[128,256]{1,0:T(8,128)(2,1)S(1)}, bf16[128,256]{1,0:T(8,128)(2,1)}, u32[]{:S(2)}) copy-start(bf16[128,256]{1,0:T(8,128)(2,1)} %get-tuple-element.6) | copy-start | bytes 196612
  144.7 24.3 %copy-start.17 = (bf16[128,256]{1,0:T(8,128)(2,1)S(1)}, bf16[128,256]{1,0:T(8,128)(2,1)}, u32[]{:S(2)}) copy-start(bf16[128,256]{1,0:T(8,128)(2,1)} %get-tuple-element.7) | copy-start | bytes 196612
  144.7 24.3 %collective-permute-start.6 = (bf16[2560,256]{1,0:T(8,128)(2,1)}, bf16[2560,256]{1,0:T(8,128)(2,1)S(1)}, u32[]{:S(2)}, u32[]{:S(2)}) collective-permute-start(bf16[2560,256]{1,0:T(8,128)(2,1)} %convolution_convert_fusion), channel_id=1, source_target_pairs={{0,1},{1,0},{2,3},{3,2},{4,5},{5,4},{6,7},{7,6},{8,9},{9,8},{10,11... | collective-permute-start | bytes 3932168 | tf_op jit(solution)/shard_map/ppermute | solution.py:100
  154.9 13.4 %collective-permute-start.7 = (bf16[8,2560]{1,0:T(8,128)(2,1)S(1)}, bf16[8,2560]{1,0:T(8,128)(2,1)S(1)}, u32[]{:S(2)}, u32[]{:S(2)}) collective-permute-start(bf16[8,2560]{1,0:T(8,128)(2,1)S(1)} %get-tuple-element.11), channel_id=1, source_target_pairs={{0,496},{16,480},{32,464},{48,448},{64,432},{80,416},{96,400},{112... | collective-permute-start | bytes 122888 | tf_op jit(solution)/shard_map/ppermute | solution.py:82

commit v2 on v1

v2 whole, which is shorter than its diff:
```python
import functools

import jax
import jax.numpy as jnp
from jax import lax
from jax.experimental import pallas as pl
from jax.experimental.pallas import tpu as pltpu
from jax.sharding import PartitionSpec as P

slope_c = 0.7978845608028654
cubic_c = 0.044715
bf16, f32 = jnp.bfloat16, jnp.float32
vmem = pltpu.CompilerParams(vmem_limit_bytes=48 * 2**20)


def gelu_both(pre):
    inner = slope_c * (pre + cubic_c * pre * pre * pre)
    tanh_v = jnp.tanh(inner)
    slope = 0.5 * (1.0 + tanh_v) + 0.5 * pre * (1.0 - tanh_v * tanh_v) * slope_c * (
        1.0 + 3.0 * cubic_c * pre * pre
    )
    return 0.5 * pre * (1.0 + tanh_v), slope


def dot(a, b, over):
    return lax.dot_general(a, b, ((over[:1], over[1:]), ((), ())), preferred_element_type=f32)


def of_kind(value, rows, kind):
    split = value.reshape(-1, 2, rows // 2, value.shape[-1])
    return split[:, kind].reshape(-1, value.shape[-1])


def merged(value):
    return value.reshape(-1, value.shape[-1])


def tick_kernel(last, where_ref, cot_ref, w_own, w_other, pre_own, pre_other, extra_ref, out_ref):
    depth = w_own.shape[1]
    tokens = pre_own.shape[2]
    chips, rows = cot_ref.shape[0], cot_ref.shape[-2]
    cot = merged(cot_ref[:, 0]) if last else merged(cot_ref[...])
    dz = []
    for w, pre in ((w_own, pre_own), (w_other, pre_other)):
        slope = gelu_both(pre[0, 0].astype(f32))[1]
        dh = dot(cot, w[0], (1, 0))
        dz.append(((dh if last else of_kind(dh, rows, 0)) * slope).astype(bf16))
    step = 512
    for start in range(0, depth, step):
        at = pl.ds(start, step)
        part = dot(dz[0], w_own[0, at, :], (1, 1)) + dot(dz[1], w_other[0, at, :], (1, 1))
        if last:
            chip = lax.broadcasted_iota(jnp.int32, part.shape, 0) // rows
            part = part + jnp.where(chip == where_ref[1], merged(cot_ref[:, 0, :, at]).astype(f32), 0.0)
            out_ref[:, at] = part.astype(bf16)
        else:
            out_ref[:, 0, :, at] = part.astype(bf16).reshape(out_ref.shape[0], -1, step)
    if not last:
        for chip in range(out_ref.shape[0]):
            out_ref[chip, 1] = extra_ref[...]


def tick_call(tick, where, cot, own_w, other_w, own_pre, other_pre, extra):
    depth, width = own_w.shape[1:]
    tokens, rows = own_pre.shape[2], extra.shape[0]
    last = tick == 1
    w_spec = pl.BlockSpec((1, depth, width), lambda i, at: (at[0], 0, 0))
    pre_spec = pl.BlockSpec((1, 1, tokens, width), lambda i, at: (at[0], tick, 0, 0))
    cot_shape = cot.shape[:1] + (1,) + cot.shape[2:] if last else cot.shape
    shape = (tokens, depth) if last else (tokens // rows, 2, rows, depth)
    return pl.pallas_call(
        functools.partial(tick_kernel, last),
        out_shape=jax.ShapeDtypeStruct(shape, bf16),
        grid_spec=pltpu.PrefetchScalarGridSpec(
            num_scalar_prefetch=1,
            grid=(1,),
            in_specs=[
                pl.BlockSpec(cot_shape, lambda i, at: (0,) * len(cot_shape)),
                w_spec, w_spec, pre_spec, pre_spec,
                pl.BlockSpec((rows, depth), lambda i, at: (0, 0)),
            ],
            out_specs=pl.BlockSpec(shape, lambda i, at: (0,) * len(shape)),
        ),
        compiler_params=vmem,
        cost_estimate=pl.CostEstimate(
            flops=8 * tokens * depth * width, bytes_accessed=10 * depth * width, transcendentals=2 * tokens * width
        ),
    )(where, cot, own_w, other_w, own_pre, other_pre, extra)


def grad_kernel(
    where_ref, one_ref, mid_ref, two_ref, swap_a, swap_b, w_own, w_other, pre_own, pre_other, pre_far, own_ref, other_ref
):
    first = where_ref[0] == 0
    depth = own_ref.shape[0]
    width = own_ref.shape[1]
    tokens, rows = swap_a.shape[0], one_ref.shape[-2]

    def left_one(at):
        return jnp.where(first, merged(one_ref[:, :, at]), jnp.concatenate([merged(mid_ref[:, 1, :, at]), swap_a[:, at]]))

    cot_one = left_one(slice(None))
    cot_two = jnp.where(first, merged(two_ref[:, 0]), merged(two_ref[:, 1]))
    rights = []
    for side, (w, pre) in enumerate(((w_own, pre_own), (w_other, pre_other))):
        (hid_one, slope_one), (hid_two, slope_two) = (
            gelu_both(jnp.where(first, pre[0, tick], pre_far[side, tick]).astype(f32)) for tick in range(2)
        )
        dh = dot(cot_one, w[0], (1, 0))
        dz_one = jnp.where(first, of_kind(dh, rows, 0), dh[:tokens]) * slope_one
        dz_two = dot(cot_two, w[0], (1, 0)) * slope_two
        in_turn = jnp.stack([value.reshape(-1, rows // 2, width) for value in (hid_one, dz_one)], 1)
        pair = jnp.where(first, in_turn.reshape(-1, width), jnp.concatenate([hid_one, dz_one]))
        rights.append(jnp.concatenate([pair.astype(bf16), dz_two.astype(bf16), hid_two.astype(bf16)]))
    right = jnp.concatenate(rights, axis=1)
    step = 256
    for start in range(0, depth, step):
        at = pl.ds(start, step)
        left = [
            cot_one[:, start : start + step],
            jnp.where(first, swap_a[:, at], swap_b[:, at]),
            cot_two[:, start : start + step],
        ]
        acc = dot(jnp.concatenate(left, axis=0), right, (0, 0)).astype(bf16)
        own_ref[at, :] = acc[:, :width]
        other_ref[at, :] = acc[:, width:]


def grad_call(where, one, mid, two, swap_a, swap_b, own_w, other_w, own_pre, other_pre, far_pre):
    depth, width = own_w.shape[1:]

    def whole(value, shape=None):
        return pl.BlockSpec(shape or value.shape, lambda i, at: (0,) * value.ndim)

    w_shape, pre_shape = (1,) + own_w.shape[1:], (1,) + own_pre.shape[1:]
    out = jax.ShapeDtypeStruct((depth, width), bf16)
    return pl.pallas_call(
        grad_kernel,
        out_shape=(out, out),
        grid_spec=pltpu.PrefetchScalarGridSpec(
            num_scalar_prefetch=1,
            grid=(1,),
            in_specs=[
                whole(one), whole(mid), whole(two), whole(swap_a), whole(swap_b),
                whole(own_w, w_shape), whole(other_w, w_shape),
                whole(own_pre, pre_shape), whole(other_pre, pre_shape), whole(far_pre),
            ],
            out_specs=(whole(out), whole(out)),
        ),
        compiler_params=vmem,
        cost_estimate=pl.CostEstimate(
            flops=12 * 256 * depth * width, bytes_accessed=16 * depth * width, transcendentals=1 << 17
        ),
    )(where, one, mid, two, swap_a, swap_b, own_w, other_w, own_pre, other_pre, far_pre)


def body(weight, stash_in, stash_pre, grad_in, grad_loss):
    sections = lax.axis_size("section")
    tensors = lax.axis_size("tensor")
    chips = tensors // 2
    end = sections - 1
    place = lax.axis_index("section")
    chip = lax.axis_index("tensor") // 2
    core = lax.axis_index("tensor") % 2
    where = jnp.stack([core, chip]).astype(jnp.int32)
    swap = [(t, t ^ 1) for t in range(tensors)]
    same_core = [[2 * j + c for j in range(chips)] for c in range(2)]
    pairs = ("section", "tensor")

    def pick(zero, one):
        return jnp.where(core == 0, zero, one)

    def moves(zero, one, flip=0):
        out = []
        for t in range(tensors):
            out += [(a * tensors + t, b * tensors + (t ^ flip)) for a, b in (one if t % 2 else zero)]
        return out

    def exchange(blocks):
        return lax.all_to_all(blocks, "tensor", 0, 0, tiled=True, axis_index_groups=same_core)

    def to_chips(rows):
        return jnp.broadcast_to(rows[None], (chips,) + rows.shape)

    def both_cores(kept, came):
        return pick(jnp.concatenate([kept, came], -2), jnp.concatenate([came, kept], -2))

    mirror = [(s, end - s) for s in range(sections)]
    down = [(s, s - 1) for s in range(1, sections)]
    up = [(s, s + 1) for s in range(end)]
    home_up = [(s, end - (s + 1)) for s in range(end)]

    own_w, own_pre = weight[0], stash_pre[0]
    x, g = stash_in[0], grad_in[0]

    n, depth = g.shape[1:]

    for_cores = jnp.stack([jnp.concatenate([g[p], x[0, p]]) for p in range(2)])
    one = lax.all_to_all(
        jnp.broadcast_to(for_cores[None], (chips,) + for_cores.shape).reshape(tensors, 2 * n, depth),
        "tensor", 0, 0, tiled=True,
    )
    other_w = lax.ppermute(own_w, "tensor", swap)
    other_pre = lax.ppermute(own_pre, "tensor", swap)

    far_g = jnp.stack([g[1], g[1]])
    far_a = lax.ppermute(pick(x[1], far_g), pairs, moves(mirror, mirror))
    far_b = lax.ppermute(pick(far_g, x[1]), pairs, moves(mirror, mirror, 1))
    far = both_cores(far_a, far_b)
    far_pre = lax.ppermute(jnp.stack([own_pre[1], other_pre[1]]), pairs, moves([], mirror))
    loss = both_cores(
        pick(grad_loss[0], grad_loss[1]), lax.ppermute(pick(grad_loss[1], grad_loss[0]), "tensor", swap)
    )

    part = tick_call(0, where, one, own_w, other_w, own_pre, other_pre, far[0])
    mid = exchange(part)
    mid, far_pre, loss = lax.optimization_barrier((mid, far_pre, loss))

    mine = lax.dynamic_slice_in_dim(one, 2 * chip, 2, 0)[:, :n].reshape(2 * n, depth)
    dx = (jnp.sum(mid[:, 0].astype(f32), axis=0) + mine.astype(f32)).astype(bf16)
    next_g = lax.ppermute(dx, pairs, moves(down, up))
    next_far = lax.ppermute(dx, pairs, moves([], home_up))
    next_g = jnp.where(place == pick(end, 0), loss, next_g)
    next_far = pick(far[1], jnp.where(place == end, loss, next_far))
    two = exchange(to_chips(jnp.stack([next_g, next_far])))
    swap_a = lax.ppermute(merged(pick(mid[:, 1], one[:, n:].reshape(mid[:, 1].shape))), "tensor", swap)
    two, swap_a = lax.optimization_barrier((two, swap_a))

    part = tick_call(1, where, two, own_w, other_w, own_pre, other_pre, far[1])
    part, late = lax.optimization_barrier((part, two))
    blocks = lax.all_to_all(part.reshape(tensors, n, depth), "tensor", 0, 0, tiled=True)
    swap_b = lax.ppermute(merged(late[:, 1]), "tensor", [(t, t + 1) for t in range(0, tensors, 2)])
    own, other = grad_call(where, one, mid, late, swap_a, swap_b, own_w, other_w, own_pre, other_pre, far_pre)
    blocks, own, other = lax.optimization_barrier((blocks, own, other))
    theirs = lax.ppermute(other, "tensor", swap)
    grad_out = jnp.sum(blocks.reshape(chips, 2, n, depth).astype(f32), axis=0).astype(bf16)[None]
    total = (own.astype(f32) + theirs.astype(f32)).astype(bf16)
    return total[None], grad_out


def solution(mesh):
    return jax.shard_map(
        body,
        mesh=mesh,
        in_specs=(
            P("section", None, None, "tensor"),
            P("section", None, None, "tensor", None),
            P("section", None, None, None, "tensor"),
            P("section", None, "tensor", None),
            P(None, "tensor", None),
        ),
        out_specs=(P("section", None, "tensor"), P("section", None, "tensor", None)),
        check_vma=False,
    )
```

time: 174 us -> 148 us (0.85)
  blocking collectives: 23.5 us -> 0 us
  starting transfers between devices: 77.2 us -> 58.1 us
  matrix products: 18.9 us -> 0 us
  Pallas kernels: 0 us -> 13.6 us
  waiting for transfers between devices: 40.8 us -> 48.6 us
  other arithmetic: 3.39 us -> 10.6 us
  local copies, waits for them, and re-layouts: 7.64 us -> 14.1 us
    all_to_all x1 -> x0, blocking collectives: 23.5 us -> none  [sum_rows(): lax.all_to_all(part.reshape(tensors, n, -1), 'tensor', 0, 0, tiled=True)]
    ppermute x7 -> x10, starting transfers between devices: 53.2 us -> 32.2 us  [the longest x1 11.5 us: body(): far_a = lax.ppermute(pick(x[1], far_g), pairs, moves(mirror, mirror))]
    dot_general x10 -> x0, matrix products: 18.9 us -> none  [dot(): lax.dot_general(a, b, ((over[:1], over[1:]), ((), ())), preferred_element...]
    pallas_call x0 -> x3, Pallas kernels: none -> 13.6 us  [the longest x2 7.44 us: tick_call(): pl.pallas_call(functools.partial(tick_kernel, last), out_shape=jax.ShapeD...]
    all_to_all x4, waiting for transfers between devices: 20.7 us -> 31.1 us  [the longest x2 27.6 us: exchange(): lax.all_to_all(blocks, 'tensor', 0, 0, tiled=True, axis_index_groups=same...]
    unnamed x36 -> x28, local copies, waits for them, and re-layouts: 0.75 us -> 6.69 us
    slice x1 -> x5, local copies, waits for them, and re-layouts: 0.01 us -> 4.21 us  [the longest x1 2.01 us: body(): mid[:, 1]]
    reduce_sum x2, other arithmetic: 0.18 us -> 3.02 us  [the longest x1 1.83 us: body(): jnp.sum(blocks.reshape(chips, 2, n, depth).astype(f32), axis=0).astype(bf16)]
  transfers between devices with their start and end apart: 12 -> 15, of which waited for: 6 -> 9; matrix products, arithmetic and copies ran while one was open for 11% -> 7% of each run, Pallas kernels for 0% -> 4%
where the time goes in v2:
time: 148 us; the launch traced here: 146 us
  starting transfers between devices  58.1 us (39%)
  waiting for transfers between devices  48.6 us (33%)
  local copies, waits for them, and re-layouts  14.1 us (10%)
  Pallas kernels  13.6 us (9%)
  other arithmetic  10.6 us (7%)
    all_to_all x2, waiting for transfers between devices, exchange(): lax.all_to_all(blocks, 'tensor', 0, 0, tiled=True, axis_index_groups=same...  27.6 us
    all_to_all x2, starting transfers between devices, exchange(): lax.all_to_all(blocks, 'tensor', 0, 0, tiled=True, axis_index_groups=same...  12.3 us
    ppermute x1, starting transfers between devices, body(): far_a = lax.ppermute(pick(x[1], far_g), pairs, moves(mirror, mirror))  11.5 us
    ppermute x1, waiting for transfers between devices, body(): far_b = lax.ppermute(pick(far_g, x[1]), pairs, moves(mirror, mirror, 1))  8.28 us
    all_to_all x1, starting transfers between devices, body(): lax.all_to_all(jnp.broadcast_to(for_cores[None], (chips,) + for_cores.sha...  7.45 us
    pallas_call x2, Pallas kernels, tick_call(): pl.pallas_call(functools.partial(tick_kernel, last), out_shape=jax.ShapeD...  7.44 us
    ppermute x1, starting transfers between devices, body(): lax.ppermute(merged(pick(mid[:, 1], one[:, n:].reshape(mid[:, 1].shape)))...  6.81 us
    unnamed x28, local copies, waits for them, and re-layouts  6.69 us
  transfers between devices with their start and end apart: 15, of which 9 were waited for; matrix products, arithmetic and copies ran while one was open for 7% of the time, Pallas kernels for 4%

profile of v2, /device:TPU:96, one launch (start us, length us, event | category | flops | bytes accessed | tf_op | source)
XLA Modules:
  0.0 146.1 jit_solution(2278673007719732308)
XLA Ops:
  0.6 1.9 %collective-permute-start = (bf16[2,2560,256]{2,1,0:T(8,128)(2,1)}, bf16[2,2560,256]{2,1,0:T(8,128)(2,1)}, u32[]{:S(2)}, u32[]{:S(2)}) collective-permute-start(bf16[2,2560,256]{2,1,0:T(8,128)(2,1)} %bitcast.56), channel_id=1, source_target_pairs={{0,1},{1,0},{2,3},{3,2},{4,5},{5,4},{6,7},{7,6},{8,9},{9,8},{10,11... | collective-permute-start | bytes 7864328 | tf_op jit(solution)/shard_map/ppermute | solution.py:203
  2.6 0.8 slice_bitcast_fusion.5
  3.4 0.8 slice_bitcast_fusion.7
  4.2 0.0 copy-start.12
  4.2 1.2 broadcast_in_dim.8
  5.4 7.4 %all-to-all-start = ((bf16[16,16,2560]{2,1,0:T(8,128)(2,1)}), bf16[16,16,2560]{2,1,0:T(8,128)(2,1)}, u32[]{:S(2)}, u32[]{:S(2)}) async-start(bf16[16,16,2560]{2,1,0:T(8,128)(2,1)} %bitcast.65), calls=%async_computation | async-start | bytes 2621440 | tf_op jit(solution)/shard_map/all_to_all | solution.py:199
  12.9 0.0 copy-done.12
  12.9 11.5 %collective-permute-start.2 = (bf16[2,8,2560]{2,1,0:T(8,128)(2,1)S(1)}, bf16[2,8,2560]{2,1,0:T(8,128)(2,1)S(1)}, u32[]{:S(2)}, u32[]{:S(2)}) collective-permute-start(bf16[2,8,2560]{2,1,0:T(8,128)(2,1)S(1)} %get-tuple-element.26), channel_id=1, source_target_pairs={{0,496},{16,480},{32,464},{48,448},{64,432},{80,416},{96,400},{112... | collective-permute-start | bytes 245768 | tf_op jit(solution)/shard_map/ppermute | solution.py:207
  24.4 1.9 %collective-permute-start.3 = (bf16[2,8,2560]{2,1,0:T(8,128)(2,1)S(1)}, bf16[2,8,2560]{2,1,0:T(8,128)(2,1)S(1)}, u32[]{:S(2)}, u32[]{:S(2)}) collective-permute-start(bf16[2,8,2560]{2,1,0:T(8,128)(2,1)S(1)} %get-tuple-element.27), channel_id=1, source_target_pairs={{0,497},{16,481},{32,465},{48,449},{64,433},{80,417},{96,401},{112... | collective-permute-start | bytes 245768 | tf_op jit(solution)/shard_map/ppermute | solution.py:208
  26.4 0.0 copy-done.2
  26.4 2.0 %collective-permute-start.1 = (bf16[2,2,128,256]{3,2,1,0:T(8,128)(2,1)S(1)}, bf16[2,2,128,256]{3,2,1,0:T(8,128)(2,1)S(1)}, u32[]{:S(2)}, u32[]{:S(2)}) collective-permute-start(bf16[2,2,128,256]{3,2,1,0:T(8,128)(2,1)S(1)} %bitcast.60), channel_id=1, source_target_pairs={{0,1},{1,0},{2,3},{3,2},{4,5},{5,4},{6,7},{7,6},{8,9},{9,8},{10,11... | collective-permute-start | bytes 786440 | tf_op jit(solution)/shard_map/ppermute | solution.py:204
  28.4 0.1 pad_add_fusion.where_ref
  28.5 1.6 %collective-permute-done.2 = bf16[2,8,2560]{2,1,0:T(8,128)(2,1)S(1)} collective-permute-done((bf16[2,8,2560]{2,1,0:T(8,128)(2,1)S(1)}, bf16[2,8,2560]{2,1,0:T(8,128)(2,1)S(1)}, u32[]{:S(2)}, u32[]{:S(2)}) %collective-permute-start.2) | collective-permute-done | bytes 81952 | tf_op jit(solution)/shard_map/ppermute | solution.py:207
  30.0 8.3 %collective-permute-done.3 = bf16[2,8,2560]{2,1,0:T(8,128)(2,1)S(1)} collective-permute-done((bf16[2,8,2560]{2,1,0:T(8,128)(2,1)S(1)}, bf16[2,8,2560]{2,1,0:T(8,128)(2,1)S(1)}, u32[]{:S(2)}, u32[]{:S(2)}) %collective-permute-start.3) | collective-permute-done | bytes 81952 | tf_op jit(solution)/shard_map/ppermute | solution.py:208
  38.4 0.0 copy-start.9
  38.4 0.7 copy-done.9
  39.0 0.0 collective-permute-done.1.pre_other
  39.1 0.0 all-to-all-done.cot_ref.one_ref
  39.1 0.0 collective-permute-done.w_other
  39.1 0.0 copy-done
  39.1 4.0 %shard_map.68 = bf16[8,2,16,2560]{3,2,1,0:T(8,128)(2,1)S(1)} custom-call(s32[2]{0:T(128)S(1)} %pad_add_fusion.where_ref, bf16[16,16,2560]{2,1,0:T(8,128)(2,1)} %all-to-all-done.cot_ref.one_ref, bf16[2,2560,256]{2,1,0:T(8,128)(2,1)S(1)} %bitcast.58, bf16[2,2560,256]{2,1,0:T(8,128)(2,1)} %collective-permute-done.w_other, ...), custom_call_target="tpu_custom_call" | custom-call | flops 671088640 | bytes 6553600 | tf_op jit(solution)/shard_map/pallas_call | solution.py:71
  43.1 0.0 copy-start.1
  43.1 1.0 copy-done.1
  44.1 8.0 %all-to-all-start.1 = ((bf16[8,2,16,2560]{3,2,1,0:T(8,128)(2,1)}), bf16[8,2,16,2560]{3,2,1,0:T(8,128)(2,1)}, u32[]{:S(2)}, u32[]{:S(2)}) async-start(bf16[8,2,16,2560]{3,2,1,0:T(8,128)(2,1)} %copy-done.1), calls=%async_computation.1 | async-start | bytes 2621440 | tf_op jit(solution)/shard_map/all_to_all | solution.py:180
  52.1 0.6 select_bitcast_fusion.3
  52.7 1.9 %collective-permute-start.5 = (bf16[8,2560]{1,0:T(8,128)(2,1)}, bf16[8,2560]{1,0:T(8,128)(2,1)}, u32[]{:S(2)}, u32[]{:S(2)}) collective-permute-start(bf16[8,2560]{1,0:T(8,128)(2,1)} %get-tuple-element.35), channel_id=1, source_target_pairs={{0,1},{1,0},{2,3},{3,2},{4,5},{5,4},{6,7},{7,6},{8,9},{9,8},{10,11... | collective-permute-start | bytes 122888 | tf_op jit(solution)/shard_map/ppermute | solution.py:212
  54.7 0.7 collective-permute-start.4
  55.4 0.8 collective-permute-done.5
  56.2 1.5 %maximum_select_fusion.1 = bf16[16,2560]{1,0:T(8,128)(2,1)} fusion(bf16[8,2560]{1,0:T(8,128)(2,1)} %collective-permute-done.5, bf16[8,2560]{1,0:T(8,128)(2,1)S(1)} %get-tuple-element.34, pred[]{:T(512)S(6)} %eq.8), kind=kLoop, calls=%fused_computation.18 | loop fusion | flops 368640 | bytes 163841 | tf_op jit(solution)/shard_map/jit(_where)/select_n | solution.py:171
  57.7 0.0 collective-permute-done.4.pre_far
  57.7 17.4 %all-to-all-done.1.mid_ref = bf16[8,2,16,2560]{3,2,1,0:T(8,128)(2,1)} async-done(((bf16[8,2,16,2560]{3,2,1,0:T(8,128)(2,1)}), bf16[8,2,16,2560]{3,2,1,0:T(8,128)(2,1)}, u32[]{:S(2)}, u32[]{:S(2)}) %all-to-all-start.1) | async-done | bytes 1310752 | tf_op jit(solution)/shard_map/all_to_all | solution.py:180
  75.0 1.2 convert_reduce_fusion
  76.2 1.5 %fusion.2 = bf16[16,2560]{1,0:T(8,128)(2,1)} fusion(f32[16,2560]{1,0:T(8,128)S(1)} %convert_reduce_fusion, bf16[16,16,2560]{2,1,0:T(8,128)(2,1)} %all-to-all-done.cot_ref.one_ref, s32[]{:T(128)S(6)} %select_n.105), kind=kLoop, calls=%fused_computation.10 | loop fusion | flops 122880 | bytes 327684 | tf_op jit(solution)/shard_map/convert_element_type | solution.py:220
  77.8 1.3 collective-permute-start.7
  79.1 1.9 %collective-permute-start.6 = (bf16[16,2560]{1,0:T(8,128)(2,1)}, bf16[16,2560]{1,0:T(8,128)(2,1)}, u32[]{:S(2)}, u32[]{:S(2)}) collective-permute-start(bf16[16,2560]{1,0:T(8,128)(2,1)} %fusion.2), channel_id=1, source_target_pairs={{16,0},{32,16},{48,32},{64,48},{80,64},{96,80},{112,96},{128,112},... | collective-permute-start | bytes 245768 | tf_op jit(solution)/shard_map/ppermute | solution.py:221
  81.0 0.0 copy-start.11
  81.0 2.0 %slice.77 = bf16[8,1,16,2560]{3,2,1,0:T(8,128)(2,1)} slice(bf16[8,2,16,2560]{3,2,1,0:T(8,128)(2,1)} %all-to-all-done.1.mid_ref), slice={[0:8], [1:2], [0:16], [0:2560]} | slice | bytes 1310720 | tf_op jit(solution)/shard_map/slice | solution.py:226
  83.0 0.0 collective-permute-done.7
  83.0 3.9 %collective-permute-done.6 = bf16[16,2560]{1,0:T(8,128)(2,1)} collective-permute-done((bf16[16,2560]{1,0:T(8,128)(2,1)}, bf16[16,2560]{1,0:T(8,128)(2,1)}, u32[]{:S(2)}, u32[]{:S(2)}) %collective-permute-start.6) | collective-permute-done | bytes 81952 | tf_op jit(solution)/shard_map/ppermute | solution.py:221
  86.9 0.9 select_bitcast_fusion.1
  87.9 1.2 broadcast_in_dim.9
  89.1 4.3 %all-to-all-start.2 = ((bf16[8,2,16,2560]{3,2,1,0:T(8,128)(2,1)}), bf16[8,2,16,2560]{3,2,1,0:T(8,128)(2,1)}, u32[]{:S(2)}, u32[]{:S(2)}) async-start(bf16[8,2,16,2560]{3,2,1,0:T(8,128)(2,1)} %broadcast_in_dim.9), calls=%async_computation.2 | async-start | bytes 2621440 | tf_op jit(solution)/shard_map/all_to_all | solution.py:180
  93.4 1.4 fusion.1
  94.7 6.8 %collective-permute-start.8 = (bf16[128,2560]{1,0:T(8,128)(2,1)S(1)}, bf16[128,2560]{1,0:T(8,128)(2,1)S(1)}, u32[]{:S(2)}, u32[]{:S(2)}) collective-permute-start(bf16[128,2560]{1,0:T(8,128)(2,1)S(1)} %fusion.1), channel_id=1, source_target_pairs={{0,1},{1,0},{2,3},{3,2},{4,5},{5,4},{6,7},{7,6},{8,9},{9,8},{10,11... | collective-permute-start | bytes 1966088 | tf_op jit(solution)/shard_map/ppermute | solution.py:226
  101.6 1.7 %collective-permute-done.8.swap_a = bf16[128,2560]{1,0:T(8,128)(2,1)S(1)} collective-permute-done((bf16[128,2560]{1,0:T(8,128)(2,1)S(1)}, bf16[128,2560]{1,0:T(8,128)(2,1)S(1)}, u32[]{:S(2)}, u32[]{:S(2)}) %collective-permute-start.8) | collective-permute-done | bytes 655392 | tf_op jit(solution)/shard_map/ppermute | solution.py:226
  103.3 0.9 copy-done.4
  104.2 10.2 %all-to-all-done.2.cot_ref.two_ref = bf16[8,2,16,2560]{3,2,1,0:T(8,128)(2,1)} async-done(((bf16[8,2,16,2560]{3,2,1,0:T(8,128)(2,1)}), bf16[8,2,16,2560]{3,2,1,0:T(8,128)(2,1)}, u32[]{:S(2)}, u32[]{:S(2)}) %all-to-all-start.2) | async-done | bytes 1310752 | tf_op jit(solution)/shard_map/all_to_all | solution.py:180
  114.4 3.5 %shard_map.69 = bf16[128,2560]{1,0:T(8,128)(2,1)S(1)} custom-call(s32[2]{0:T(128)S(1)} %pad_add_fusion.where_ref, bf16[8,2,16,2560]{3,2,1,0:T(8,128)(2,1)} %all-to-all-done.2.cot_ref.two_ref, bf16[2,2560,256]{2,1,0:T(8,128)(2,1)S(1)} %bitcast.59, bf16[2,2560,256]{2,1,0:T(8,128)(2,1)} %collective-permute-done.w_other, bf16[2,2,128,256]{3,2,1,0:T(8,128)(2,1)S(1)} %bitcast.62, ...), custom_call_target="tpu_custom_call" | custom-call | flops 671088640 | bytes 6553600 | tf_op jit(solution)/shard_map/pallas_call | solution.py:71
  117.8 1.4 slice.79
  119.2 2.3 %collective-permute-start.9 = (bf16[128,2560]{1,0:T(8,128)(2,1)S(1)}, bf16[128,2560]{1,0:T(8,128)(2,1)S(1)}, u32[]{:S(2)}, u32[]{:S(2)}) collective-permute-start(bf16[128,2560]{1,0:T(8,128)(2,1)S(1)} %bitcast.66), channel_id=1, source_target_pairs={{0,1},{2,3},{4,5},{6,7},{8,9},{10,11},{12,13},{14,15},{16,17},{18,... | collective-permute-start | bytes 1966088 | tf_op jit(solution)/shard_map/ppermute | solution.py:232
  121.5 4.3 %all-to-all-start.3 = ((bf16[16,8,2560]{2,1,0:T(8,128)(2,1)}), bf16[16,8,2560]{2,1,0:T(8,128)(2,1)}, u32[]{:S(2)}, u32[]{:S(2)}) async-start(bf16[16,8,2560]{2,1,0:T(8,128)(2,1)} %bitcast.64), calls=%async_computation.3 | async-start | bytes 1310720 | tf_op jit(solution)/shard_map/all_to_all | solution.py:231
  125.8 0.0 collective-permute-done.9.swap_b
  125.8 0.0 copy-start.6
  125.8 0.8 copy-done.6
  126.6 1.1 copy-done.5
  127.7 1.1 copy-done.7
  128.8 6.2 %shard_map.70 = (bf16[2560,256]{1,0:T(8,128)(2,1)S(1)}, bf16[2560,256]{1,0:T(8,128)(2,1)S(1)}) custom-call(s32[2]{0:T(128)S(1)} %pad_add_fusion.where_ref, bf16[16,16,2560]{2,1,0:T(8,128)(2,1)} %all-to-all-done.cot_ref.one_ref, bf16[8,2,16,2560]{3,2,1,0:T(8,128)(2,1)} %all-to-all-done.1.mid_ref, bf16[8,2,16,2560]{3,2,1,0:T(8,128)(2,1)} %all-to-all-done.2.cot_ref.two_ref, ...), custom_call_target="tpu_custom_call" | custom-call | flops 2013265920 | bytes 10485760 | tf_op jit(solution)/shard_map/pallas_call | solution.py:137
  135.0 0.0 copy-start.8
  135.0 1.0 copy-done.8
  136.1 3.5 %all-to-all-done.3 = bf16[16,8,2560]{2,1,0:T(8,128)(2,1)} async-done(((bf16[16,8,2560]{2,1,0:T(8,128)(2,1)}), bf16[16,8,2560]{2,1,0:T(8,128)(2,1)}, u32[]{:S(2)}, u32[]{:S(2)}) %all-to-all-start.3) | async-done | bytes 655392 | tf_op jit(solution)/shard_map/all_to_all | solution.py:231
  139.6 1.9 %collective-permute-start.10 = (bf16[2560,256]{1,0:T(8,128)(2,1)}, bf16[2560,256]{1,0:T(8,128)(2,1)S(1)}, u32[]{:S(2)}, u32[]{:S(2)}) collective-permute-start(bf16[2560,256]{1,0:T(8,128)(2,1)} %copy-done.8), channel_id=1, source_target_pairs={{0,1},{1,0},{2,3},{3,2},{4,5},{5,4},{6,7},{7,6},{8,9},{9,8},{10,11... | collective-permute-start | bytes 3932168 | tf_op jit(solution)/shard_map/ppermute | solution.py:235
  141.5 1.8 %reduce_sum.22 = bf16[2,8,2560]{2,1,0:T(8,128)(2,1)} reduce(bf16[8,2,8,2560]{3,2,1,0:T(8,128)(2,1)} %bitcast.27, bf16[]{:T(256)} %constant.41.clone.1), dimensions={0}, to_apply=%region_1.2 | reduce | flops 286720 | bytes 737282 | tf_op jit(solution)/shard_map/reduce_sum | solution.py:236
  143.3 1.4 collective-permute-done.10
  144.7 1.4 fusion
  (21 shorter events, 0.2 us)
Async XLA Ops:
  0.6 38.4 %collective-permute-start = (bf16[2,2560,256]{2,1,0:T(8,128)(2,1)}, bf16[2,2560,256]{2,1,0:T(8,128)(2,1)}, u32[]{:S(2)}, u32[]{:S(2)}) collective-permute-start(bf16[2,2560,256]{2,1,0:T(8,128)(2,1)} %bitcast.56), channel_id=1, source_target_pairs={{0,1},{1,0},{2,3},{3,2},{4,5},{5,4},{6,7},{7,6},{8,9},{9,8},{10,11... | collective-permute-start | bytes 7864328 | tf_op jit(solution)/shard_map/ppermute | solution.py:203
  4.2 8.7 %copy-start.12 = (bf16[1,2,2,8,2560]{4,3,2,1,0:T(8,128)(2,1)S(1)}, bf16[1,2,2,8,2560]{4,3,2,1,0:T(8,128)(2,1)}, u32[]{:S(2)}) copy-start(bf16[1,2,2,8,2560]{4,3,2,1,0:T(8,128)(2,1)} %param.6) | copy-start | bytes 491524
  5.4 20.9 %copy-start.2 = (bf16[1,2,2,128,256]{4,3,2,1,0:T(8,128)(2,1)S(1)}, bf16[1,2,2,128,256]{4,3,2,1,0:T(8,128)(2,1)}, u32[]{:S(2)}) copy-start(bf16[1,2,2,128,256]{4,3,2,1,0:T(8,128)(2,1)} %param.7) | copy-start | bytes 786436
  5.4 33.6 %copy-start = (bf16[1,2,2560,256]{3,2,1,0:T(8,128)(2,1)S(1)}, bf16[1,2,2560,256]{3,2,1,0:T(8,128)(2,1)}, u32[]{:S(2)}) copy-start(bf16[1,2,2560,256]{3,2,1,0:T(8,128)(2,1)} %param.5) | copy-start | bytes 7864324
  5.4 33.6 %all-to-all-start = ((bf16[16,16,2560]{2,1,0:T(8,128)(2,1)}), bf16[16,16,2560]{2,1,0:T(8,128)(2,1)}, u32[]{:S(2)}, u32[]{:S(2)}) async-start(bf16[16,16,2560]{2,1,0:T(8,128)(2,1)} %bitcast.65), calls=%async_computation | async-start | bytes 2621440 | tf_op jit(solution)/shard_map/all_to_all | solution.py:199
  12.9 17.1 %collective-permute-start.2 = (bf16[2,8,2560]{2,1,0:T(8,128)(2,1)S(1)}, bf16[2,8,2560]{2,1,0:T(8,128)(2,1)S(1)}, u32[]{:S(2)}, u32[]{:S(2)}) collective-permute-start(bf16[2,8,2560]{2,1,0:T(8,128)(2,1)S(1)} %get-tuple-element.26), channel_id=1, source_target_pairs={{0,496},{16,480},{32,464},{48,448},{64,432},{80,416},{96,400},{112... | collective-permute-start | bytes 245768 | tf_op jit(solution)/shard_map/ppermute | solution.py:207
  24.4 13.9 %collective-permute-start.3 = (bf16[2,8,2560]{2,1,0:T(8,128)(2,1)S(1)}, bf16[2,8,2560]{2,1,0:T(8,128)(2,1)S(1)}, u32[]{:S(2)}, u32[]{:S(2)}) collective-permute-start(bf16[2,8,2560]{2,1,0:T(8,128)(2,1)S(1)} %get-tuple-element.27), channel_id=1, source_target_pairs={{0,497},{16,481},{32,465},{48,449},{64,433},{80,417},{96,401},{112... | collective-permute-start | bytes 245768 | tf_op jit(solution)/shard_map/ppermute | solution.py:208
  26.4 12.7 %collective-permute-start.1 = (bf16[2,2,128,256]{3,2,1,0:T(8,128)(2,1)S(1)}, bf16[2,2,128,256]{3,2,1,0:T(8,128)(2,1)S(1)}, u32[]{:S(2)}, u32[]{:S(2)}) collective-permute-start(bf16[2,2,128,256]{3,2,1,0:T(8,128)(2,1)S(1)} %bitcast.60), channel_id=1, source_target_pairs={{0,1},{1,0},{2,3},{3,2},{4,5},{5,4},{6,7},{7,6},{8,9},{9,8},{10,11... | collective-permute-start | bytes 786440 | tf_op jit(solution)/shard_map/ppermute | solution.py:204
  38.4 0.7 copy-start.9
  43.1 1.1 copy-start.1
  44.1 8.0 %copy-start.13 = (bf16[2,8,2560]{2,1,0:T(8,128)(2,1)S(1)}, bf16[2,8,2560]{2,1,0:T(8,128)(2,1)}, u32[]{:S(2)}) copy-start(bf16[2,8,2560]{2,1,0:T(8,128)(2,1)} %param.9) | copy-start | bytes 245764
  44.1 30.9 %all-to-all-start.1 = ((bf16[8,2,16,2560]{3,2,1,0:T(8,128)(2,1)}), bf16[8,2,16,2560]{3,2,1,0:T(8,128)(2,1)}, u32[]{:S(2)}, u32[]{:S(2)}) async-start(bf16[8,2,16,2560]{3,2,1,0:T(8,128)(2,1)} %copy-done.1), calls=%async_computation.1 | async-start | bytes 2621440 | tf_op jit(solution)/shard_map/all_to_all | solution.py:180
  52.7 3.4 %collective-permute-start.5 = (bf16[8,2560]{1,0:T(8,128)(2,1)}, bf16[8,2560]{1,0:T(8,128)(2,1)}, u32[]{:S(2)}, u32[]{:S(2)}) collective-permute-start(bf16[8,2560]{1,0:T(8,128)(2,1)} %get-tuple-element.35), channel_id=1, source_target_pairs={{0,1},{1,0},{2,3},{3,2},{4,5},{5,4},{6,7},{7,6},{8,9},{9,8},{10,11... | collective-permute-start | bytes 122888 | tf_op jit(solution)/shard_map/ppermute | solution.py:212
  54.7 3.0 %collective-permute-start.4 = (bf16[2,2,128,256]{3,2,1,0:T(8,128)(2,1)S(1)}, bf16[2,2,128,256]{3,2,1,0:T(8,128)(2,1)S(1)}, u32[]{:S(2)}, u32[]{:S(2)}) collective-permute-start(bf16[2,2,128,256]{3,2,1,0:T(8,128)(2,1)S(1)} %pad_maximum_fusion), channel_id=1, source_target_pairs={{1,497},{17,481},{33,465},{49,449},{65,433},{81,417},{97,401},{113... | collective-permute-start | bytes 786440 | tf_op jit(solution)/shard_map/ppermute | solution.py:210
  77.8 5.3 %collective-permute-start.7 = (bf16[16,2560]{1,0:T(8,128)(2,1)}, bf16[16,2560]{1,0:T(8,128)(2,1)}, u32[]{:S(2)}, u32[]{:S(2)}) collective-permute-start(bf16[16,2560]{1,0:T(8,128)(2,1)} %fusion.2), channel_id=1, source_target_pairs={{1,481},{17,465},{33,449},{49,433},{65,417},{81,401},{97,385},{113... | collective-permute-start | bytes 245768 | tf_op jit(solution)/shard_map/ppermute | solution.py:222
  79.1 7.9 %collective-permute-start.6 = (bf16[16,2560]{1,0:T(8,128)(2,1)}, bf16[16,2560]{1,0:T(8,128)(2,1)}, u32[]{:S(2)}, u32[]{:S(2)}) collective-permute-start(bf16[16,2560]{1,0:T(8,128)(2,1)} %fusion.2), channel_id=1, source_target_pairs={{16,0},{32,16},{48,32},{64,48},{80,64},{96,80},{112,96},{128,112},... | collective-permute-start | bytes 245768 | tf_op jit(solution)/shard_map/ppermute | solution.py:221
  81.0 5.9 %copy-start.10 = (bf16[2,16,2560]{2,1,0:T(8,128)(2,1)S(1)}, bf16[2,16,2560]{2,1,0:T(8,128)(2,1)}, u32[]{:S(2)}) copy-start(bf16[2,16,2560]{2,1,0:T(8,128)(2,1)} %copy-done.9) | copy-start | bytes 491524
  81.0 5.9 %copy-start.11 = (bf16[16,2560]{1,0:T(8,128)(2,1)S(1)}, bf16[16,2560]{1,0:T(8,128)(2,1)}, u32[]{:S(2)}) copy-start(bf16[16,2560]{1,0:T(8,128)(2,1)} %maximum_select_fusion.1) | copy-start | bytes 245764
  89.1 25.3 %all-to-all-start.2 = ((bf16[8,2,16,2560]{3,2,1,0:T(8,128)(2,1)}), bf16[8,2,16,2560]{3,2,1,0:T(8,128)(2,1)}, u32[]{:S(2)}, u32[]{:S(2)}) async-start(bf16[8,2,16,2560]{3,2,1,0:T(8,128)(2,1)} %broadcast_in_dim.9), calls=%async_computation.2 | async-start | bytes 2621440 | tf_op jit(solution)/shard_map/all_to_all | solution.py:180
  94.7 8.5 %collective-permute-start.8 = (bf16[128,2560]{1,0:T(8,128)(2,1)S(1)}, bf16[128,2560]{1,0:T(8,128)(2,1)S(1)}, u32[]{:S(2)}, u32[]{:S(2)}) collective-permute-start(bf16[128,2560]{1,0:T(8,128)(2,1)S(1)} %fusion.1), channel_id=1, source_target_pairs={{0,1},{1,0},{2,3},{3,2},{4,5},{5,4},{6,7},{7,6},{8,9},{9,8},{10,11... | collective-permute-start | bytes 1966088 | tf_op jit(solution)/shard_map/ppermute | solution.py:226
  103.3 0.9 copy-start.4
  117.8 3.7 %copy-start.3 = (bf16[128,2560]{1,0:T(8,128)(2,1)}, bf16[128,2560]{1,0:T(8,128)(2,1)S(1)}, u32[]{:S(2)}) copy-start(bf16[128,2560]{1,0:T(8,128)(2,1)S(1)} %shard_map.69) | copy-start | bytes 1966084
  119.2 6.6 %collective-permute-start.9 = (bf16[128,2560]{1,0:T(8,128)(2,1)S(1)}, bf16[128,2560]{1,0:T(8,128)(2,1)S(1)}, u32[]{:S(2)}, u32[]{:S(2)}) collective-permute-start(bf16[128,2560]{1,0:T(8,128)(2,1)S(1)} %bitcast.66), channel_id=1, source_target_pairs={{0,1},{2,3},{4,5},{6,7},{8,9},{10,11},{12,13},{14,15},{16,17},{18,... | collective-permute-start | bytes 1966088 | tf_op jit(solution)/shard_map/ppermute | solution.py:232
  121.5 18.1 %all-to-all-start.3 = ((bf16[16,8,2560]{2,1,0:T(8,128)(2,1)}), bf16[16,8,2560]{2,1,0:T(8,128)(2,1)}, u32[]{:S(2)}, u32[]{:S(2)}) async-start(bf16[16,8,2560]{2,1,0:T(8,128)(2,1)} %bitcast.64), calls=%async_computation.3 | async-start | bytes 1310720 | tf_op jit(solution)/shard_map/all_to_all | solution.py:231
  125.8 0.8 copy-start.6
  126.6 1.1 copy-start.5
  127.7 1.1 copy-start.7
  135.0 1.1 copy-start.8
  139.6 5.1 %collective-permute-start.10 = (bf16[2560,256]{1,0:T(8,128)(2,1)}, bf16[2560,256]{1,0:T(8,128)(2,1)S(1)}, u32[]{:S(2)}, u32[]{:S(2)}) collective-permute-start(bf16[2560,256]{1,0:T(8,128)(2,1)} %copy-done.8), channel_id=1, source_target_pairs={{0,1},{1,0},{2,3},{3,2},{4,5},{5,4},{6,7},{7,6},{8,9},{9,8},{10,11... | collective-permute-start | bytes 3932168 | tf_op jit(solution)/shard_map/ppermute | solution.py:235

commit v3 on v2

v3 whole, which is shorter than its diff:
```python
import functools

import jax
import jax.numpy as jnp
from jax import lax
from jax.experimental import pallas as pl
from jax.experimental.pallas import tpu as pltpu
from jax.sharding import PartitionSpec as P

slope_c = 0.7978845608028654
cubic_c = 0.044715
bf16, f32 = jnp.bfloat16, jnp.float32
vmem = pltpu.CompilerParams(vmem_limit_bytes=48 * 2**20)


def gelu_both(pre):
    inner = slope_c * (pre + cubic_c * pre * pre * pre)
    tanh_v = jnp.tanh(inner)
    slope = 0.5 * (1.0 + tanh_v) + 0.5 * pre * (1.0 - tanh_v * tanh_v) * slope_c * (
        1.0 + 3.0 * cubic_c * pre * pre
    )
    return 0.5 * pre * (1.0 + tanh_v), slope


def dot(a, b, over):
    return lax.dot_general(a, b, ((over[:1], over[1:]), ((), ())), preferred_element_type=f32)


def of_kind(value, rows, kind):
    split = value.reshape(-1, 2, rows // 2, value.shape[-1])
    return split[:, kind].reshape(-1, value.shape[-1])


def merged(value):
    return value.reshape(-1, value.shape[-1])


def tick_kernel(last, where_ref, cot_ref, w_own, w_other, pre_own, pre_other, out_ref):
    chips, rows, depth = out_ref.shape
    turn = cot_ref.shape[-2]
    cot = merged(cot_ref[:, 0]) if last else merged(cot_ref[...])
    dz = []
    for w, pre in ((w_own, pre_own), (w_other, pre_other)):
        slope = gelu_both(pre[0, 0].astype(f32))[1]
        dh = dot(cot, w[0], (1, 0))
        dz.append(((dh if last else of_kind(dh, turn, 0)) * slope).astype(bf16))
    step = 512
    for start in range(0, depth, step):
        at = pl.ds(start, step)
        part = dot(dz[0], w_own[0, at, :], (1, 1)) + dot(dz[1], w_other[0, at, :], (1, 1))
        chip = lax.broadcasted_iota(jnp.int32, part.shape, 0) // rows
        added = cot[:, start : start + step].astype(f32)
        part = part + jnp.where(chip == where_ref[1], added if last else of_kind(added, turn, 0), 0.0)
        out_ref[:, :, at] = part.astype(bf16).reshape(chips, rows, step)


def tick_call(tick, where, cot, own_w, other_w, own_pre, other_pre):
    depth, width = own_w.shape[1:]
    tokens = own_pre.shape[2]
    rows = 16
    w_specs = [pl.BlockSpec((1, depth, width), lambda i, at, own=own: (at[0] * own, 0, 0)) for own in (1, 0)]
    pre_specs = [pl.BlockSpec((1, 1, tokens, width), lambda i, at, own=own: (at[0] * own, tick, 0, 0)) for own in (1, 0)]
    cot_shape = cot.shape[:1] + (1,) + cot.shape[2:] if tick == 1 else cot.shape
    shape = (tokens // rows, rows, depth)
    return pl.pallas_call(
        functools.partial(tick_kernel, tick == 1),
        out_shape=pltpu.HBM(shape, bf16),
        grid_spec=pltpu.PrefetchScalarGridSpec(
            num_scalar_prefetch=1,
            grid=(1,),
            in_specs=[
                pl.BlockSpec(cot_shape, lambda i, at: (0,) * len(cot_shape)),
                *w_specs, *pre_specs,
            ],
            out_specs=pl.BlockSpec(shape, lambda i, at: (0,) * len(shape)),
        ),
        compiler_params=vmem,
        cost_estimate=pl.CostEstimate(
            flops=8 * tokens * depth * width, bytes_accessed=10 * depth * width, transcendentals=2 * tokens * width
        ),
    )(where, cot, own_w, other_w, own_pre, other_pre)


def grad_kernel(where_ref, one_ref, one_came, two_ref, two_came, w_ref, pre_near, pre_far, out_ref):
    depth, width = out_ref.shape
    tokens, turn = pre_near.shape[2], one_ref.shape[-2]

    def in_turn(kinds):
        return jnp.stack([kind.reshape(-1, turn // 2, width) for kind in kinds], 1).reshape(-1, width).astype(bf16)

    def form(one_a, one_b, two_a, two_b):
        w = w_ref[0]
        (hid_1, slope_1), (hid_2, slope_2) = (gelu_both(pre_near[0, tick].astype(f32)) for tick in range(2))
        dz_1 = of_kind(dot(merged(one_a[...]), w, (1, 0)), turn, 0) * slope_1
        dz_2 = dot(merged(two_a[:, 0]), w, (1, 0)) * slope_2
        right_near = jnp.concatenate([in_turn((hid_1, dz_1)), in_turn((jnp.zeros_like(dz_2), dz_2)), hid_2.astype(bf16)])
        rights = []
        for tick in range(2):
            hid, slope = gelu_both(pre_far[0, tick].astype(f32))
            dz = dot(merged(two_b[:, 1 + tick]), w, (1, 0)) * slope
            rights += [dz.astype(bf16), hid.astype(bf16)]
        right_far = jnp.concatenate(rights)
        step = 256
        for start in range(0, depth, step):
            at = pl.ds(start, step)
            left = jnp.concatenate([merged(one_a[:, :, at]), merged(one_b[:, :, at]), merged(two_a[:, 0, :, at])])
            near = dot(left, right_near, (0, 0)).astype(bf16)
            left = jnp.concatenate(
                [merged(ref[:, 1 + tick, :, at]) for tick in range(2) for ref in (two_a, two_b)]
            )
            far = dot(left, right_far, (0, 0)).astype(bf16)
            out_ref[at, :] = (near.astype(f32) + far.astype(f32)).astype(bf16)

    @pl.when(where_ref[0] == 0)
    def _():
        form(one_ref, one_came, two_ref, two_came)

    @pl.when(where_ref[0] == 1)
    def _():
        form(one_came, one_ref, two_came, two_ref)


def grad_call(where, one, one_came, two, two_came, own_w, own_pre, far_pre):
    depth, width = own_w.shape[1:]

    def whole(value, shape=None):
        return pl.BlockSpec(shape or value.shape, lambda i, at: (0,) * value.ndim)

    out = jax.ShapeDtypeStruct((depth, width), bf16)
    return pl.pallas_call(
        grad_kernel,
        out_shape=out,
        grid_spec=pltpu.PrefetchScalarGridSpec(
            num_scalar_prefetch=1,
            grid=(1,),
            in_specs=[
                whole(one), whole(one_came), whole(two), whole(two_came), whole(own_w, (1,) + own_w.shape[1:]),
                whole(own_pre, (1,) + own_pre.shape[1:]), whole(far_pre),
            ],
            out_specs=whole(out),
        ),
        compiler_params=vmem,
        cost_estimate=pl.CostEstimate(
            flops=12 * 256 * depth * width, bytes_accessed=16 * depth * width, transcendentals=1 << 17
        ),
    )(where, one, one_came, two, two_came, own_w, own_pre, far_pre)


def body(weight, stash_in, stash_pre, grad_in, grad_loss):
    sections = lax.axis_size("section")
    tensors = lax.axis_size("tensor")
    chips = tensors // 2
    end = sections - 1
    place = lax.axis_index("section")
    chip = lax.axis_index("tensor") // 2
    core = lax.axis_index("tensor") % 2
    where = jnp.stack([core, chip]).astype(jnp.int32)
    swap = [(t, t ^ 1) for t in range(tensors)]
    same_core = [[2 * j + c for j in range(chips)] for c in range(2)]
    pairs = ("section", "tensor")

    def pick(zero, one):
        return jnp.where(core == 0, zero, one)

    def moves(zero, one, flip=0):
        out = []
        for t in range(tensors):
            out += [(a * tensors + t, b * tensors + (t ^ flip)) for a, b in (one if t % 2 else zero)]
        return out

    def exchange(blocks):
        return lax.all_to_all(blocks, "tensor", 0, 0, tiled=True, axis_index_groups=same_core)

    def to_chips(rows):
        return jnp.broadcast_to(rows[None], (chips,) + rows.shape)

    def both_cores(kept, came):
        return pick(jnp.concatenate([kept, came], -2), jnp.concatenate([came, kept], -2))

    mirror = [(s, end - s) for s in range(sections)]
    down = [(s, s - 1) for s in range(1, sections)]
    up = [(s, s + 1) for s in range(end)]
    home_up = [(s, end - (s + 1)) for s in range(end)]

    own_w, own_pre = weight[0], stash_pre[0]
    x, g = stash_in[0], grad_in[0]

    n, depth = g.shape[1:]

    for_cores = jnp.stack([jnp.concatenate([g[p], x[0, p]]) for p in range(2)])
    one = lax.all_to_all(
        jnp.broadcast_to(for_cores[None], (chips,) + for_cores.shape).reshape(tensors, 2 * n, depth),
        "tensor", 0, 0, tiled=True,
    )
    other_w = lax.ppermute(pick(own_w[1:], own_w[:1]), "tensor", swap)
    other_pre = lax.ppermute(pick(own_pre[1:], own_pre[:1]), "tensor", swap)

    far_g = jnp.stack([g[1], g[1]])
    far_a = lax.ppermute(pick(x[1], far_g), pairs, moves(mirror, mirror))
    far_b = lax.ppermute(pick(far_g, x[1]), pairs, moves(mirror, mirror, 1))
    far = both_cores(far_a, far_b)
    far_pre = lax.ppermute(own_pre[1:], "section", mirror)

    part = tick_call(0, where, one, own_w, other_w, own_pre, other_pre)
    mid = exchange(part)
    mid, far = lax.optimization_barrier((mid, far))

    begin = place == pick(end, 0)
    last_sends = place == pick(0, end)
    dx = jnp.sum(mid.astype(f32), axis=0).astype(bf16)
    own_loss, for_other = pick(grad_loss[0], grad_loss[1]), pick(grad_loss[1], grad_loss[0])
    doubled = jnp.concatenate([for_other, for_other])
    at_end = [(end * tensors + t, end * tensors + t + 1) for t in range(0, tensors, 2)]
    at_ends = [(t, t + 1) for t in range(0, tensors, 2)] + [(b, a) for a, b in at_end]
    next_far = lax.ppermute(pick(doubled, dx), pairs, moves([], home_up) + at_end)
    next_g = lax.ppermute(jnp.where(last_sends, doubled, dx), pairs, moves(down, up) + at_ends)
    next_g = jnp.where(begin, both_cores(own_loss, next_g[:n]), next_g)
    next_far = pick(far[1], jnp.where(place == end, both_cores(own_loss, next_far[:n]), next_far))
    two = exchange(to_chips(jnp.stack([next_g, far[0], next_far])))
    one_came = lax.ppermute(one, "tensor", swap)
    two, one_came, far_pre = lax.optimization_barrier((two, one_came, far_pre))

    part = tick_call(1, where, two, own_w, other_w, own_pre, other_pre)
    part, late = lax.optimization_barrier((part, two))
    blocks = lax.all_to_all(part.reshape(tensors, n, depth), "tensor", 0, 0, tiled=True)
    two_came = lax.ppermute(late, "tensor", swap)
    total = grad_call(where, one, one_came, late, two_came, own_w, own_pre, far_pre)
    blocks, total = lax.optimization_barrier((blocks, total))
    grad_out = jnp.sum(blocks.reshape(chips, 2, n, depth).astype(f32), axis=0).astype(bf16)[None]
    return total[None], grad_out


def solution(mesh):
    return jax.shard_map(
        body,
        mesh=mesh,
        in_specs=(
            P("section", None, None, "tensor"),
            P("section", None, None, "tensor", None),
            P("section", None, None, None, "tensor"),
            P("section", None, "tensor", None),
            P(None, "tensor", None),
        ),
        out_specs=(P("section", None, "tensor"), P("section", None, "tensor", None)),
        check_vma=False,
    )
```

time: 148 us -> 132 us (0.89)
  the two profiles are of different devices: /device:TPU:96 before, /device:TPU:8 now
where the time goes in v3:
time: 132 us; the launch traced here: 131 us
  starting transfers between devices  61.8 us (47%)
  waiting for transfers between devices  42.9 us (32%)
  Pallas kernels  16.3 us (12%)
  local copies, waits for them, and re-layouts  5.14 us (4%)
  other arithmetic  4.1 us (3%)
    all_to_all x2, waiting for transfers between devices, exchange(): lax.all_to_all(blocks, 'tensor', 0, 0, tiled=True, axis_index_groups=same...  16.8 us
    ppermute x1, waiting for transfers between devices, body(): far_pre = lax.ppermute(own_pre[1:], 'section', mirror)  14.9 us
    ppermute x1, starting transfers between devices, body(): lax.ppermute(jnp.where(last_sends, doubled, dx), pairs, moves(down, up) +...  13.3 us
    ppermute x1, starting transfers between devices, body(): far_a = lax.ppermute(pick(x[1], far_g), pairs, moves(mirror, mirror))  12.2 us
    pallas_call x2, Pallas kernels, tick_call(): pl.pallas_call(functools.partial(tick_kernel, tick == 1), out_shape=pltpu...  9.4 us
    all_to_all x2, starting transfers between devices, exchange(): lax.all_to_all(blocks, 'tensor', 0, 0, tiled=True, axis_index_groups=same...  7.27 us
    pallas_call x1, Pallas kernels, grad_call(): pl.pallas_call(grad_kernel, out_shape=out, grid_spec=pltpu.PrefetchScalar...  6.86 us
    all_to_all x1, starting transfers between devices, body(): lax.all_to_all(jnp.broadcast_to(for_cores[None], (chips,) + for_cores.sha...  6.55 us
  transfers between devices with their start and end apart: 13, of which 6 were waited for; matrix products, arithmetic and copies ran while one was open for 1% of the time, Pallas kernels for 9%

profile of v3, /device:TPU:8, one launch (start us, length us, event | category | flops | bytes accessed | tf_op | source)
XLA Modules:
  0.0 131.2 jit_solution(438607230751970103)
XLA Ops:
  0.6 0.0 copy-start.4
  0.7 0.0 copy-start.5
  0.7 3.0 %select_bitcast_fusion = bf16[1,2560,256]{2,1,0:T(8,128)(2,1)} fusion(bf16[1,2,2560,256]{3,2,1,0:T(8,128)(2,1)} %param.5, pred[]{:T(512)S(6)} %eq.10), kind=kLoop, calls=%fused_computation | loop fusion | flops 655360 | bytes 3932161 | tf_op jit(solution)/shard_map/jit(_where)/select_n | solution.py:163
  3.6 1.9 %collective-permute-start = (bf16[1,2560,256]{2,1,0:T(8,128)(2,1)}, bf16[1,2560,256]{2,1,0:T(8,128)(2,1)}, u32[]{:S(2)}, u32[]{:S(2)}) collective-permute-start(bf16[1,2560,256]{2,1,0:T(8,128)(2,1)} %select_bitcast_fusion), channel_id=1, source_target_pairs={{0,1},{1,0},{2,3},{3,2},{4,5},{5,4},{6,7},{7,6},{8,9},{9,8},{10,11... | collective-permute-start | bytes 3932168 | tf_op jit(solution)/shard_map/ppermute | solution.py:195
  5.5 0.0 copy-done.4
  5.6 0.0 copy-done.5
  5.6 0.0 copy-start.1
  5.7 1.2 broadcast_in_dim.8
  6.8 0.0 copy-start
  6.8 6.5 %all-to-all-start = ((bf16[16,16,2560]{2,1,0:T(8,128)(2,1)}), bf16[16,16,2560]{2,1,0:T(8,128)(2,1)}, u32[]{:S(2)}, u32[]{:S(2)}) async-start(bf16[16,16,2560]{2,1,0:T(8,128)(2,1)} %bitcast.51), calls=%async_computation | async-start | bytes 2621440 | tf_op jit(solution)/shard_map/all_to_all | solution.py:191
  13.4 0.0 copy-done.1
  13.4 2.3 %collective-permute-start.1 = (bf16[1,2,128,256]{3,2,1,0:T(8,128)(2,1)S(1)}, bf16[1,2,128,256]{3,2,1,0:T(8,128)(2,1)S(1)}, u32[]{:S(2)}, u32[]{:S(2)}) collective-permute-start(bf16[1,2,128,256]{3,2,1,0:T(8,128)(2,1)S(1)} %bitcast_select_fusion), channel_id=1, source_target_pairs={{0,1},{1,0},{2,3},{3,2},{4,5},{5,4},{6,7},{7,6},{8,9},{9,8},{10,11... | collective-permute-start | bytes 393224 | tf_op jit(solution)/shard_map/ppermute | solution.py:196
  15.7 12.2 %collective-permute-start.2 = (bf16[2,8,2560]{2,1,0:T(8,128)(2,1)S(1)}, bf16[2,8,2560]{2,1,0:T(8,128)(2,1)S(1)}, u32[]{:S(2)}, u32[]{:S(2)}) collective-permute-start(bf16[2,8,2560]{2,1,0:T(8,128)(2,1)S(1)} %get-tuple-element.20), channel_id=1, source_target_pairs={{0,496},{16,480},{32,464},{48,448},{64,432},{80,416},{96,400},{112... | collective-permute-start | bytes 245768 | tf_op jit(solution)/shard_map/ppermute | solution.py:199
  27.9 1.9 %collective-permute-start.3 = (bf16[2,8,2560]{2,1,0:T(8,128)(2,1)S(1)}, bf16[2,8,2560]{2,1,0:T(8,128)(2,1)S(1)}, u32[]{:S(2)}, u32[]{:S(2)}) collective-permute-start(bf16[2,8,2560]{2,1,0:T(8,128)(2,1)S(1)} %get-tuple-element.21), channel_id=1, source_target_pairs={{0,497},{16,481},{32,465},{48,449},{64,433},{80,417},{96,401},{112... | collective-permute-start | bytes 245768 | tf_op jit(solution)/shard_map/ppermute | solution.py:200
  29.9 0.1 pad_add_fusion.where_ref
  29.9 0.0 collective-permute-done.1.pre_other
  30.0 4.3 %all-to-all-done.cot_ref.one_ref = bf16[16,16,2560]{2,1,0:T(8,128)(2,1)} async-done(((bf16[16,16,2560]{2,1,0:T(8,128)(2,1)}), bf16[16,16,2560]{2,1,0:T(8,128)(2,1)}, u32[]{:S(2)}, u32[]{:S(2)}) %all-to-all-start) | async-done | bytes 1310752 | tf_op jit(solution)/shard_map/all_to_all | solution.py:191
  34.2 0.0 collective-permute-done.w_other
  34.3 0.0 copy-done
  34.3 4.8 %shard_map.68 = bf16[8,16,2560]{2,1,0:T(8,128)(2,1)} custom-call(s32[2]{0:T(128)S(1)} %pad_add_fusion.where_ref, bf16[16,16,2560]{2,1,0:T(8,128)(2,1)} %all-to-all-done.cot_ref.one_ref, bf16[2,2560,256]{2,1,0:T(8,128)(2,1)S(1)} %bitcast.47, bf16[1,2560,256]{2,1,0:T(8,128)(2,1)} %collective-permute-done.w_other, bf16[2,2,128,256]{3,2,1,0:T(8,128)(2,1)S(1)} %bitcast.48, ...), custom_call_target="tpu_custom_call" | custom-call | flops 671088640 | bytes 6553600 | tf_op jit(solution)/shard_map/pallas_call | solution.py:65
  39.1 0.0 copy-start.6
  39.1 3.7 %all-to-all-start.1 = ((bf16[8,16,2560]{2,1,0:T(8,128)(2,1)}), bf16[8,16,2560]{2,1,0:T(8,128)(2,1)S(1)}, u32[]{:S(2)}, u32[]{:S(2)}) async-start(bf16[8,16,2560]{2,1,0:T(8,128)(2,1)} %shard_map.68), calls=%async_computation.1 | async-start | bytes 1310720 | tf_op jit(solution)/shard_map/all_to_all | solution.py:172
  42.8 0.0 copy-done.6
  42.8 0.0 collective-permute-done.2
  42.8 0.0 collective-permute-done.3
  42.9 13.1 %all-to-all-done.1 = bf16[8,16,2560]{2,1,0:T(8,128)(2,1)S(1)} async-done(((bf16[8,16,2560]{2,1,0:T(8,128)(2,1)}), bf16[8,16,2560]{2,1,0:T(8,128)(2,1)S(1)}, u32[]{:S(2)}, u32[]{:S(2)}) %all-to-all-start.1) | async-done | bytes 655392 | tf_op jit(solution)/shard_map/all_to_all | solution.py:172
  55.9 0.1 reduce_sum.24
  56.1 13.3 %collective-permute-start.4 = (bf16[16,2560]{1,0:T(8,128)(2,1)S(1)}, bf16[16,2560]{1,0:T(8,128)(2,1)S(1)}, u32[]{:S(2)}, u32[]{:S(2)}) collective-permute-start(bf16[16,2560]{1,0:T(8,128)(2,1)S(1)} %get-tuple-element.24), channel_id=1, source_target_pairs={{16,0},{32,16},{48,32},{64,48},{80,64},{96,80},{112,96},{128,112},... | collective-permute-start | bytes 245768 | tf_op jit(solution)/shard_map/ppermute | solution.py:216
  69.4 0.7 collective-permute-start.5
  70.1 1.3 %collective-permute-done.4 = bf16[16,2560]{1,0:T(8,128)(2,1)S(1)} collective-permute-done((bf16[16,2560]{1,0:T(8,128)(2,1)S(1)}, bf16[16,2560]{1,0:T(8,128)(2,1)S(1)}, u32[]{:S(2)}, u32[]{:S(2)}) %collective-permute-start.4) | collective-permute-done | bytes 81952 | tf_op jit(solution)/shard_map/ppermute | solution.py:216
  71.4 0.0 collective-permute-done.5
  71.5 0.1 fusion.2
  71.6 1.5 %broadcast_in_dim.9 = bf16[8,3,16,2560]{3,2,1,0:T(8,128)(2,1)} broadcast(bf16[3,16,2560]{2,1,0:T(8,128)(2,1)S(1)} %pad_maximum_fusion), dimensions={1,2,3} | broadcast | bytes 2211840 | tf_op jit(solution)/shard_map/broadcast_in_dim | solution.py:175
  73.1 3.6 %all-to-all-start.2 = ((bf16[8,3,16,2560]{3,2,1,0:T(8,128)(2,1)}), bf16[8,3,16,2560]{3,2,1,0:T(8,128)(2,1)S(1)}, u32[]{:S(2)}, u32[]{:S(2)}) async-start(bf16[8,3,16,2560]{3,2,1,0:T(8,128)(2,1)} %broadcast_in_dim.9), calls=%async_computation.2 | async-start | bytes 3932160 | tf_op jit(solution)/shard_map/all_to_all | solution.py:172
  76.7 6.1 %collective-permute-start.6 = (bf16[16,16,2560]{2,1,0:T(8,128)(2,1)}, bf16[16,16,2560]{2,1,0:T(8,128)(2,1)S(1)}, u32[]{:S(2)}, u32[]{:S(2)}) collective-permute-start(bf16[16,16,2560]{2,1,0:T(8,128)(2,1)} %all-to-all-done.cot_ref.one_ref), channel_id=1, source_target_pairs={{0,1},{1,0},{2,3},{3,2},{4,5},{5,4},{6,7},{7,6},{8,9},{9,8},{10,11... | collective-permute-start | bytes 3932168 | tf_op jit(solution)/shard_map/ppermute | solution.py:220
  82.8 2.2 %collective-permute-start.7 = (bf16[1,2,128,256]{3,2,1,0:T(8,128)(2,1)S(1)}, bf16[1,2,128,256]{3,2,1,0:T(8,128)(2,1)S(1)}, u32[]{:S(2)}, u32[]{:S(2)}) collective-permute-start(bf16[1,2,128,256]{3,2,1,0:T(8,128)(2,1)S(1)} %slice_bitcast_fusion), channel_id=1, source_target_pairs={{0,496},{16,480},{32,464},{48,448},{64,432},{80,416},{96,400},{112... | collective-permute-start | bytes 393224 | tf_op jit(solution)/shard_map/ppermute | solution.py:202
  85.0 14.9 %collective-permute-done.7.pre_far = bf16[1,2,128,256]{3,2,1,0:T(8,128)(2,1)S(1)} collective-permute-done((bf16[1,2,128,256]{3,2,1,0:T(8,128)(2,1)S(1)}, bf16[1,2,128,256]{3,2,1,0:T(8,128)(2,1)S(1)}, u32[]{:S(2)}, u32[]{:S(2)}) %collective-permute-start.7) | collective-permute-done | bytes 131104 | tf_op jit(solution)/shard_map/ppermute | solution.py:202
  99.9 0.0 collective-permute-done.6.one_came
  99.9 0.0 copy-start.2
  99.9 1.1 copy-done.2
  101.0 3.8 %all-to-all-done.2.cot_ref.two_ref = bf16[8,3,16,2560]{3,2,1,0:T(8,128)(2,1)S(1)} async-done(((bf16[8,3,16,2560]{3,2,1,0:T(8,128)(2,1)}), bf16[8,3,16,2560]{3,2,1,0:T(8,128)(2,1)S(1)}, u32[]{:S(2)}, u32[]{:S(2)}) %all-to-all-start.2) | async-done | bytes 1966112 | tf_op jit(solution)/shard_map/all_to_all | solution.py:172
  104.7 4.6 %shard_map.69 = bf16[8,16,2560]{2,1,0:T(8,128)(2,1)} custom-call(s32[2]{0:T(128)S(1)} %pad_add_fusion.where_ref, bf16[8,3,16,2560]{3,2,1,0:T(8,128)(2,1)S(1)} %all-to-all-done.2.cot_ref.two_ref, bf16[2,2560,256]{2,1,0:T(8,128)(2,1)} %bitcast.45, bf16[1,2560,256]{2,1,0:T(8,128)(2,1)} %collective-permute-done.w_other, bf16[2,2,128,256]{3,2,1,0:T(8,128)(2,1)S(1)} %bitcast.49, ...), custom_call_target="tpu_custom_call" | custom-call | flops 671088640 | bytes 6553600 | tf_op jit(solution)/shard_map/pallas_call | solution.py:65
  109.3 3.3 %collective-permute-start.8 = (bf16[8,3,16,2560]{3,2,1,0:T(8,128)(2,1)S(1)}, bf16[8,3,16,2560]{3,2,1,0:T(8,128)(2,1)}, u32[]{:S(2)}, u32[]{:S(2)}) collective-permute-start(bf16[8,3,16,2560]{3,2,1,0:T(8,128)(2,1)S(1)} %all-to-all-done.2.cot_ref.two_ref), channel_id=1, source_target_pairs={{0,1},{1,0},{2,3},{3,2},{4,5},{5,4},{6,7},{7,6},{8,9},{9,8},{10,11... | collective-permute-start | bytes 5898248 | tf_op jit(solution)/shard_map/ppermute | solution.py:226
  112.6 4.1 %all-to-all-start.3 = ((bf16[16,8,2560]{2,1,0:T(8,128)(2,1)}), bf16[16,8,2560]{2,1,0:T(8,128)(2,1)S(1)}, u32[]{:S(2)}, u32[]{:S(2)}) async-start(bf16[16,8,2560]{2,1,0:T(8,128)(2,1)} %bitcast.53), calls=%async_computation.3 | async-start | bytes 1310720 | tf_op jit(solution)/shard_map/all_to_all | solution.py:225
  116.7 0.0 collective-permute-done.8.two_came
  116.7 0.0 copy-start.3
  116.7 1.3 copy-done.3
  118.1 6.9 %shard_map.70 = bf16[2560,256]{1,0:T(8,128)(2,1)} custom-call(s32[2]{0:T(128)S(1)} %pad_add_fusion.where_ref, bf16[16,16,2560]{2,1,0:T(8,128)(2,1)} %all-to-all-done.cot_ref.one_ref, bf16[16,16,2560]{2,1,0:T(8,128)(2,1)S(1)} %copy-done.3, bf16[8,3,16,2560]{3,2,1,0:T(8,128)(2,1)S(1)} %all-to-all-done.2.cot_ref.two_ref, ...), custom_call_target="tpu_custom_call" | custom-call | flops 2013265920 | bytes 10485760 | tf_op jit(solution)/shard_map/pallas_call | solution.py:130
  124.9 5.6 %all-to-all-done.3 = bf16[16,8,2560]{2,1,0:T(8,128)(2,1)S(1)} async-done(((bf16[16,8,2560]{2,1,0:T(8,128)(2,1)}), bf16[16,8,2560]{2,1,0:T(8,128)(2,1)S(1)}, u32[]{:S(2)}, u32[]{:S(2)}) %all-to-all-start.3) | async-done | bytes 655392 | tf_op jit(solution)/shard_map/all_to_all | solution.py:225
  130.5 0.7 reduce_sum.25
  (14 shorter events, 0.2 us)
Async XLA Ops:
  0.6 4.9 %copy-start.4 = (bf16[1,2,2,8,2560]{4,3,2,1,0:T(8,128)(2,1)S(1)}, bf16[1,2,2,8,2560]{4,3,2,1,0:T(8,128)(2,1)}, u32[]{:S(2)}) copy-start(bf16[1,2,2,8,2560]{4,3,2,1,0:T(8,128)(2,1)} %param.6) | copy-start | bytes 491524
  0.7 4.9 %copy-start.5 = (bf16[1,2,8,2560]{3,2,1,0:T(8,128)(2,1)S(1)}, bf16[1,2,8,2560]{3,2,1,0:T(8,128)(2,1)}, u32[]{:S(2)}) copy-start(bf16[1,2,8,2560]{3,2,1,0:T(8,128)(2,1)} %param.8) | copy-start | bytes 245764
  3.6 30.6 %collective-permute-start = (bf16[1,2560,256]{2,1,0:T(8,128)(2,1)}, bf16[1,2560,256]{2,1,0:T(8,128)(2,1)}, u32[]{:S(2)}, u32[]{:S(2)}) collective-permute-start(bf16[1,2560,256]{2,1,0:T(8,128)(2,1)} %select_bitcast_fusion), channel_id=1, source_target_pairs={{0,1},{1,0},{2,3},{3,2},{4,5},{5,4},{6,7},{7,6},{8,9},{9,8},{10,11... | collective-permute-start | bytes 3932168 | tf_op jit(solution)/shard_map/ppermute | solution.py:195
  5.6 7.8 %copy-start.1 = (bf16[1,2,2,128,256]{4,3,2,1,0:T(8,128)(2,1)S(1)}, bf16[1,2,2,128,256]{4,3,2,1,0:T(8,128)(2,1)}, u32[]{:S(2)}) copy-start(bf16[1,2,2,128,256]{4,3,2,1,0:T(8,128)(2,1)} %param.7) | copy-start | bytes 786436
  6.8 27.4 %copy-start = (bf16[1,2,2560,256]{3,2,1,0:T(8,128)(2,1)S(1)}, bf16[1,2,2560,256]{3,2,1,0:T(8,128)(2,1)}, u32[]{:S(2)}) copy-start(bf16[1,2,2560,256]{3,2,1,0:T(8,128)(2,1)} %param.5) | copy-start | bytes 7864324
  6.8 27.4 %all-to-all-start = ((bf16[16,16,2560]{2,1,0:T(8,128)(2,1)}), bf16[16,16,2560]{2,1,0:T(8,128)(2,1)}, u32[]{:S(2)}, u32[]{:S(2)}) async-start(bf16[16,16,2560]{2,1,0:T(8,128)(2,1)} %bitcast.51), calls=%async_computation | async-start | bytes 2621440 | tf_op jit(solution)/shard_map/all_to_all | solution.py:191
  13.4 16.5 %collective-permute-start.1 = (bf16[1,2,128,256]{3,2,1,0:T(8,128)(2,1)S(1)}, bf16[1,2,128,256]{3,2,1,0:T(8,128)(2,1)S(1)}, u32[]{:S(2)}, u32[]{:S(2)}) collective-permute-start(bf16[1,2,128,256]{3,2,1,0:T(8,128)(2,1)S(1)} %bitcast_select_fusion), channel_id=1, source_target_pairs={{0,1},{1,0},{2,3},{3,2},{4,5},{5,4},{6,7},{7,6},{8,9},{9,8},{10,11... | collective-permute-start | bytes 393224 | tf_op jit(solution)/shard_map/ppermute | solution.py:196
  15.7 27.1 %collective-permute-start.2 = (bf16[2,8,2560]{2,1,0:T(8,128)(2,1)S(1)}, bf16[2,8,2560]{2,1,0:T(8,128)(2,1)S(1)}, u32[]{:S(2)}, u32[]{:S(2)}) collective-permute-start(bf16[2,8,2560]{2,1,0:T(8,128)(2,1)S(1)} %get-tuple-element.20), channel_id=1, source_target_pairs={{0,496},{16,480},{32,464},{48,448},{64,432},{80,416},{96,400},{112... | collective-permute-start | bytes 245768 | tf_op jit(solution)/shard_map/ppermute | solution.py:199
  27.9 14.9 %collective-permute-start.3 = (bf16[2,8,2560]{2,1,0:T(8,128)(2,1)S(1)}, bf16[2,8,2560]{2,1,0:T(8,128)(2,1)S(1)}, u32[]{:S(2)}, u32[]{:S(2)}) collective-permute-start(bf16[2,8,2560]{2,1,0:T(8,128)(2,1)S(1)} %get-tuple-element.21), channel_id=1, source_target_pairs={{0,497},{16,481},{32,465},{48,449},{64,433},{80,417},{96,401},{112... | collective-permute-start | bytes 245768 | tf_op jit(solution)/shard_map/ppermute | solution.py:200
  39.1 3.7 %copy-start.6 = (bf16[2,8,2560]{2,1,0:T(8,128)(2,1)S(1)}, bf16[2,8,2560]{2,1,0:T(8,128)(2,1)}, u32[]{:S(2)}) copy-start(bf16[2,8,2560]{2,1,0:T(8,128)(2,1)} %param.9) | copy-start | bytes 245764
  39.1 16.8 %all-to-all-start.1 = ((bf16[8,16,2560]{2,1,0:T(8,128)(2,1)}), bf16[8,16,2560]{2,1,0:T(8,128)(2,1)S(1)}, u32[]{:S(2)}, u32[]{:S(2)}) async-start(bf16[8,16,2560]{2,1,0:T(8,128)(2,1)} %shard_map.68), calls=%async_computation.1 | async-start | bytes 1310720 | tf_op jit(solution)/shard_map/all_to_all | solution.py:172
  56.1 15.4 %collective-permute-start.4 = (bf16[16,2560]{1,0:T(8,128)(2,1)S(1)}, bf16[16,2560]{1,0:T(8,128)(2,1)S(1)}, u32[]{:S(2)}, u32[]{:S(2)}) collective-permute-start(bf16[16,2560]{1,0:T(8,128)(2,1)S(1)} %get-tuple-element.24), channel_id=1, source_target_pairs={{16,0},{32,16},{48,32},{64,48},{80,64},{96,80},{112,96},{128,112},... | collective-permute-start | bytes 245768 | tf_op jit(solution)/shard_map/ppermute | solution.py:216
  69.4 2.0 %collective-permute-start.5 = (bf16[16,2560]{1,0:T(8,128)(2,1)S(1)}, bf16[16,2560]{1,0:T(8,128)(2,1)S(1)}, u32[]{:S(2)}, u32[]{:S(2)}) collective-permute-start(bf16[16,2560]{1,0:T(8,128)(2,1)S(1)} %get-tuple-element.25), channel_id=1, source_target_pairs={{1,481},{17,465},{33,449},{49,433},{65,417},{81,401},{97,385},{113... | collective-permute-start | bytes 245768 | tf_op jit(solution)/shard_map/ppermute | solution.py:215
  73.1 31.6 %all-to-all-start.2 = ((bf16[8,3,16,2560]{3,2,1,0:T(8,128)(2,1)}), bf16[8,3,16,2560]{3,2,1,0:T(8,128)(2,1)S(1)}, u32[]{:S(2)}, u32[]{:S(2)}) async-start(bf16[8,3,16,2560]{3,2,1,0:T(8,128)(2,1)} %broadcast_in_dim.9), calls=%async_computation.2 | async-start | bytes 3932160 | tf_op jit(solution)/shard_map/all_to_all | solution.py:172
  76.7 23.2 %collective-permute-start.6 = (bf16[16,16,2560]{2,1,0:T(8,128)(2,1)}, bf16[16,16,2560]{2,1,0:T(8,128)(2,1)S(1)}, u32[]{:S(2)}, u32[]{:S(2)}) collective-permute-start(bf16[16,16,2560]{2,1,0:T(8,128)(2,1)} %all-to-all-done.cot_ref.one_ref), channel_id=1, source_target_pairs={{0,1},{1,0},{2,3},{3,2},{4,5},{5,4},{6,7},{7,6},{8,9},{9,8},{10,11... | collective-permute-start | bytes 3932168 | tf_op jit(solution)/shard_map/ppermute | solution.py:220
  82.8 17.1 %collective-permute-start.7 = (bf16[1,2,128,256]{3,2,1,0:T(8,128)(2,1)S(1)}, bf16[1,2,128,256]{3,2,1,0:T(8,128)(2,1)S(1)}, u32[]{:S(2)}, u32[]{:S(2)}) collective-permute-start(bf16[1,2,128,256]{3,2,1,0:T(8,128)(2,1)S(1)} %slice_bitcast_fusion), channel_id=1, source_target_pairs={{0,496},{16,480},{32,464},{48,448},{64,432},{80,416},{96,400},{112... | collective-permute-start | bytes 393224 | tf_op jit(solution)/shard_map/ppermute | solution.py:202
  99.9 1.1 copy-start.2
  109.3 7.4 %collective-permute-start.8 = (bf16[8,3,16,2560]{3,2,1,0:T(8,128)(2,1)S(1)}, bf16[8,3,16,2560]{3,2,1,0:T(8,128)(2,1)}, u32[]{:S(2)}, u32[]{:S(2)}) collective-permute-start(bf16[8,3,16,2560]{3,2,1,0:T(8,128)(2,1)S(1)} %all-to-all-done.2.cot_ref.two_ref), channel_id=1, source_target_pairs={{0,1},{1,0},{2,3},{3,2},{4,5},{5,4},{6,7},{7,6},{8,9},{9,8},{10,11... | collective-permute-start | bytes 5898248 | tf_op jit(solution)/shard_map/ppermute | solution.py:226
  112.6 17.9 %all-to-all-start.3 = ((bf16[16,8,2560]{2,1,0:T(8,128)(2,1)}), bf16[16,8,2560]{2,1,0:T(8,128)(2,1)S(1)}, u32[]{:S(2)}, u32[]{:S(2)}) async-start(bf16[16,8,2560]{2,1,0:T(8,128)(2,1)} %bitcast.53), calls=%async_computation.3 | async-start | bytes 1310720 | tf_op jit(solution)/shard_map/all_to_all | solution.py:225
  116.7 1.3 %copy-start.3 = (bf16[16,16,2560]{2,1,0:T(8,128)(2,1)S(1)}, bf16[16,16,2560]{2,1,0:T(8,128)(2,1)}, u32[]{:S(2)}) copy-start(bf16[16,16,2560]{2,1,0:T(8,128)(2,1)} %copy-done.2) | copy-start | bytes 3932164

commit v4 on v3

--- a/solution.py
+++ b/solution.py
@@ -35,19 +35,22 @@
     return value.reshape(-1, value.shape[-1])
 
 
-def tick_kernel(last, where_ref, cot_ref, w_own, w_other, pre_own, pre_other, out_ref):
+def tick_kernel(last, where_ref, cot_ref, w_own, *refs):
+    *w_halves, pre_own, pre_other, out_ref = refs
     chips, rows, depth = out_ref.shape
     turn = cot_ref.shape[-2]
+    half = depth // 2
     cot = merged(cot_ref[:, 0]) if last else merged(cot_ref[...])
+    dh_own = dot(cot, w_own[0], (1, 0))
+    dh_other = sum(dot(cot[:, k * half : (k + 1) * half], w[0], (1, 0)) for k, w in enumerate(w_halves))
     dz = []
-    for w, pre in ((w_own, pre_own), (w_other, pre_other)):
+    for dh, pre in ((dh_own, pre_own), (dh_other, pre_other)):
         slope = gelu_both(pre[0, 0].astype(f32))[1]
-        dh = dot(cot, w[0], (1, 0))
         dz.append(((dh if last else of_kind(dh, turn, 0)) * slope).astype(bf16))
-    step = 512
+    step = half // 2
     for start in range(0, depth, step):
-        at = pl.ds(start, step)
-        part = dot(dz[0], w_own[0, at, :], (1, 1)) + dot(dz[1], w_other[0, at, :], (1, 1))
+        at, inside = pl.ds(start, step), pl.ds(start % half, step)
+        part = dot(dz[0], w_own[0, at, :], (1, 1)) + dot(dz[1], w_halves[start // half][0, inside, :], (1, 1))
         chip = lax.broadcasted_iota(jnp.int32, part.shape, 0) // rows
         added = cot[:, start : start + step].astype(f32)
         part = part + jnp.where(chip == where_ref[1], added if last else of_kind(added, turn, 0), 0.0)
@@ -58,7 +61,8 @@
     depth, width = own_w.shape[1:]
     tokens = own_pre.shape[2]
     rows = 16
-    w_specs = [pl.BlockSpec((1, depth, width), lambda i, at, own=own: (at[0] * own, 0, 0)) for own in (1, 0)]
+    w_specs = [pl.BlockSpec((1, depth, width), lambda i, at: (at[0], 0, 0))]
+    w_specs += [pl.BlockSpec(w.shape, lambda i, at: (0, 0, 0)) for w in other_w]
     pre_specs = [pl.BlockSpec((1, 1, tokens, width), lambda i, at, own=own: (at[0] * own, tick, 0, 0)) for own in (1, 0)]
     cot_shape = cot.shape[:1] + (1,) + cot.shape[2:] if tick == 1 else cot.shape
     shape = (tokens // rows, rows, depth)
@@ -78,7 +82,7 @@
         cost_estimate=pl.CostEstimate(
             flops=8 * tokens * depth * width, bytes_accessed=10 * depth * width, transcendentals=2 * tokens * width
         ),
-    )(where, cot, own_w, other_w, own_pre, other_pre)
+    )(where, cot, own_w, *other_w, own_pre, other_pre)
 
 
 def grad_kernel(where_ref, one_ref, one_came, two_ref, two_came, w_ref, pre_near, pre_far, out_ref):
@@ -192,7 +196,13 @@
         jnp.broadcast_to(for_cores[None], (chips,) + for_cores.shape).reshape(tensors, 2 * n, depth),
         "tensor", 0, 0, tiled=True,
     )
-    other_w = lax.ppermute(pick(own_w[1:], own_w[:1]), "tensor", swap)
+    half = depth // 2
+    other_w = [
+        lax.ppermute(
+            lax.dynamic_slice(own_w, (1 - core, k * half, 0), (1, half, own_w.shape[2])), "tensor", swap
+        )
+        for k in range(2)
+    ]
     other_pre = lax.ppermute(pick(own_pre[1:], own_pre[:1]), "tensor", swap)
 
     far_g = jnp.stack([g[1], g[1]])

time: 132 us -> 131 us (level)
  the two profiles are of different devices: /device:TPU:8 before, /device:TPU:96 now
where the time goes in v4:
time: 131 us; the launch traced here: 130 us
  starting transfers between devices  68.4 us (52%)
  waiting for transfers between devices  31.7 us (24%)
  Pallas kernels  15.7 us (12%)
  local copies, waits for them, and re-layouts  8.48 us (6%)
  other arithmetic  5.19 us (4%)
    ppermute x1, starting transfers between devices, body(): one_came = lax.ppermute(one, 'tensor', swap)  13.2 us
    ppermute x1, starting transfers between devices, body(): far_a = lax.ppermute(pick(x[1], far_g), pairs, moves(mirror, mirror))  11.5 us
    all_to_all x2, waiting for transfers between devices, exchange(): lax.all_to_all(blocks, 'tensor', 0, 0, tiled=True, axis_index_groups=same...  11.4 us
    all_to_all x2, starting transfers between devices, exchange(): lax.all_to_all(blocks, 'tensor', 0, 0, tiled=True, axis_index_groups=same...  11.1 us
    ppermute x1, waiting for transfers between devices, body(): far_pre = lax.ppermute(own_pre[1:], 'section', mirror)  9.89 us
    pallas_call x2, Pallas kernels, tick_call(): pl.pallas_call(functools.partial(tick_kernel, tick == 1), out_shape=pltpu...  8.83 us
    all_to_all x1, starting transfers between devices, body(): lax.all_to_all(jnp.broadcast_to(for_cores[None], (chips,) + for_cores.sha...  7.21 us
    pallas_call x1, Pallas kernels, grad_call(): pl.pallas_call(grad_kernel, out_shape=out, grid_spec=pltpu.PrefetchScalar...  6.86 us
  transfers between devices with their start and end apart: 14, of which 4 were waited for; matrix products, arithmetic and copies ran while one was open for 4% of the time, Pallas kernels for 9%

profile of v4, /device:TPU:96, one launch (start us, length us, event | category | flops | bytes accessed | tf_op | source)
XLA Modules:
  0.0 130.3 jit_solution(6170012374229838848)
XLA Ops:
  0.6 0.8 slice_bitcast_fusion.2
  1.4 1.4 %slice_bitcast_fusion.4 = (bf16[1,8,2560]{2,1,0:T(8,128)(2,1)}, bf16[8,2560]{1,0:T(8,128)(2,1)S(1)}, bf16[8,2560]{1,0:T(8,128)(2,1)S(1)}) fusion(bf16[1,2,8,2560]{3,2,1,0:T(8,128)(2,1)} %param.8), kind=kLoop, calls=%fused_computation.31 | loop fusion | bytes 204800 | tf_op jit(solution)/shard_map/slice | solution.py:194
  2.9 0.0 copy-start.1
  2.9 0.0 copy-start
  2.9 1.2 broadcast_in_dim.8
  4.1 7.2 %all-to-all-start = ((bf16[16,16,2560]{2,1,0:T(8,128)(2,1)}), bf16[16,16,2560]{2,1,0:T(8,128)(2,1)}, u32[]{:S(2)}, u32[]{:S(2)}) async-start(bf16[16,16,2560]{2,1,0:T(8,128)(2,1)} %bitcast.53), calls=%async_computation | async-start | bytes 2621440 | tf_op jit(solution)/shard_map/all_to_all | solution.py:195
  11.3 0.0 copy-done.1
  11.4 0.7 bitcast_select_fusion
  12.0 2.2 %collective-permute-start.2 = (bf16[1,2,128,256]{3,2,1,0:T(8,128)(2,1)}, bf16[1,2,128,256]{3,2,1,0:T(8,128)(2,1)}, u32[]{:S(2)}, u32[]{:S(2)}) collective-permute-start(bf16[1,2,128,256]{3,2,1,0:T(8,128)(2,1)} %bitcast_select_fusion), channel_id=1, source_target_pairs={{0,1},{1,0},{2,3},{3,2},{4,5},{5,4},{6,7},{7,6},{8,9},{9,8},{10,11... | collective-permute-start | bytes 393224 | tf_op jit(solution)/shard_map/ppermute | solution.py:206
  14.3 0.0 copy-done
  14.3 1.2 dynamic-slice_bitcast_fusion
  15.5 2.1 %collective-permute-start.1 = (bf16[1,1280,256]{2,1,0:T(8,128)(2,1)}, bf16[1,1280,256]{2,1,0:T(8,128)(2,1)S(1)}, u32[]{:S(2)}, u32[]{:S(2)}) collective-permute-start(bf16[1,1280,256]{2,1,0:T(8,128)(2,1)} %get-tuple-element.20), channel_id=1, source_target_pairs={{0,1},{1,0},{2,3},{3,2},{4,5},{5,4},{6,7},{7,6},{8,9},{9,8},{10,11... | collective-permute-start | bytes 1966088 | tf_op jit(solution)/shard_map/ppermute | solution.py:201
  17.5 2.3 %collective-permute-start = (bf16[1,1280,256]{2,1,0:T(8,128)(2,1)}, bf16[1,1280,256]{2,1,0:T(8,128)(2,1)}, u32[]{:S(2)}, u32[]{:S(2)}) collective-permute-start(bf16[1,1280,256]{2,1,0:T(8,128)(2,1)} %get-tuple-element.21), channel_id=1, source_target_pairs={{0,1},{1,0},{2,3},{3,2},{4,5},{5,4},{6,7},{7,6},{8,9},{9,8},{10,11... | collective-permute-start | bytes 1966088 | tf_op jit(solution)/shard_map/ppermute | solution.py:201
  19.8 1.6 %bitcast_select_fusion.2 = (bf16[2,8,2560]{2,1,0:T(8,128)(2,1)}, bf16[2,8,2560]{2,1,0:T(8,128)(2,1)}) fusion(pred[]{:T(512)S(6)} %eq.10, bf16[1,8,2560]{2,1,0:T(8,128)(2,1)} %get-tuple-element.30, bf16[1,2,2,8,2560]{4,3,2,1,0:T(8,128)(2,1)} %param.6), kind=kLoop, calls=%fused_computation.23 | loop fusion | flops 122880 | bytes 286721 | tf_op jit(solution)/shard_map/jit(_where)/select_n | solution.py:167
  21.4 11.5 %collective-permute-start.3 = (bf16[2,8,2560]{2,1,0:T(8,128)(2,1)}, bf16[2,8,2560]{2,1,0:T(8,128)(2,1)}, u32[]{:S(2)}, u32[]{:S(2)}) collective-permute-start(bf16[2,8,2560]{2,1,0:T(8,128)(2,1)} %get-tuple-element.22), channel_id=1, source_target_pairs={{0,496},{16,480},{32,464},{48,448},{64,432},{80,416},{96,400},{112... | collective-permute-start | bytes 245768 | tf_op jit(solution)/shard_map/ppermute | solution.py:209
  32.9 1.9 %collective-permute-start.4 = (bf16[2,8,2560]{2,1,0:T(8,128)(2,1)}, bf16[2,8,2560]{2,1,0:T(8,128)(2,1)}, u32[]{:S(2)}, u32[]{:S(2)}) collective-permute-start(bf16[2,8,2560]{2,1,0:T(8,128)(2,1)} %get-tuple-element.23), channel_id=1, source_target_pairs={{0,497},{16,481},{32,465},{48,449},{64,433},{80,417},{96,401},{112... | collective-permute-start | bytes 245768 | tf_op jit(solution)/shard_map/ppermute | solution.py:210
  34.8 0.1 pad_add_fusion.where_ref
  34.9 0.0 collective-permute-done.2.refs_3_
  34.9 0.0 collective-permute-done.1.refs_1_
  34.9 0.0 collective-permute-done.refs_0_
  34.9 0.0 all-to-all-done.cot_ref.one_ref
  34.9 4.6 %shard_map.68 = bf16[8,16,2560]{2,1,0:T(8,128)(2,1)} custom-call(s32[2]{0:T(128)S(1)} %pad_add_fusion.where_ref, bf16[16,16,2560]{2,1,0:T(8,128)(2,1)} %all-to-all-done.cot_ref.one_ref, bf16[2,2560,256]{2,1,0:T(8,128)(2,1)S(1)} %bitcast.49, bf16[1,1280,256]{2,1,0:T(8,128)(2,1)} %collective-permute-done.refs_0_, ...), custom_call_target="tpu_custom_call" | custom-call | flops 671088640 | bytes 6553600 | tf_op jit(solution)/shard_map/pallas_call | solution.py:69
  39.5 7.5 %all-to-all-start.1 = ((bf16[8,16,2560]{2,1,0:T(8,128)(2,1)}), bf16[8,16,2560]{2,1,0:T(8,128)(2,1)S(1)}, u32[]{:S(2)}, u32[]{:S(2)}) async-start(bf16[8,16,2560]{2,1,0:T(8,128)(2,1)} %shard_map.68), calls=%async_computation.1 | async-start | bytes 1310720 | tf_op jit(solution)/shard_map/all_to_all | solution.py:176
  47.0 0.8 select_bitcast_fusion.1
  47.8 0.0 collective-permute-done.3
  47.8 0.0 collective-permute-done.4
  47.8 1.0 maximum_select_fusion
  48.9 11.4 %all-to-all-done.1 = bf16[8,16,2560]{2,1,0:T(8,128)(2,1)S(1)} async-done(((bf16[8,16,2560]{2,1,0:T(8,128)(2,1)}), bf16[8,16,2560]{2,1,0:T(8,128)(2,1)S(1)}, u32[]{:S(2)}, u32[]{:S(2)}) %all-to-all-start.1) | async-done | bytes 655392 | tf_op jit(solution)/shard_map/all_to_all | solution.py:176
  60.2 0.1 reduce_sum.24
  60.4 2.0 %collective-permute-start.5 = (bf16[16,2560]{1,0:T(8,128)(2,1)S(1)}, bf16[16,2560]{1,0:T(8,128)(2,1)S(1)}, u32[]{:S(2)}, u32[]{:S(2)}) collective-permute-start(bf16[16,2560]{1,0:T(8,128)(2,1)S(1)} %get-tuple-element.26), channel_id=1, source_target_pairs={{16,0},{32,16},{48,32},{64,48},{80,64},{96,80},{112,96},{128,112},... | collective-permute-start | bytes 245768 | tf_op jit(solution)/shard_map/ppermute | solution.py:226
  62.4 0.7 collective-permute-start.6
  63.1 4.8 %collective-permute-done.5 = bf16[16,2560]{1,0:T(8,128)(2,1)S(1)} collective-permute-done((bf16[16,2560]{1,0:T(8,128)(2,1)S(1)}, bf16[16,2560]{1,0:T(8,128)(2,1)S(1)}, u32[]{:S(2)}, u32[]{:S(2)}) %collective-permute-start.5) | collective-permute-done | bytes 81952 | tf_op jit(solution)/shard_map/ppermute | solution.py:226
  67.9 0.0 collective-permute-done.6
  67.9 0.1 fusion.2
  68.0 1.5 %broadcast_in_dim.9 = bf16[8,3,16,2560]{3,2,1,0:T(8,128)(2,1)} broadcast(bf16[3,16,2560]{2,1,0:T(8,128)(2,1)S(1)} %pad_maximum_fusion), dimensions={1,2,3} | broadcast | bytes 2211840 | tf_op jit(solution)/shard_map/broadcast_in_dim | solution.py:179
  69.5 3.6 %all-to-all-start.2 = ((bf16[8,3,16,2560]{3,2,1,0:T(8,128)(2,1)}), bf16[8,3,16,2560]{3,2,1,0:T(8,128)(2,1)S(1)}, u32[]{:S(2)}, u32[]{:S(2)}) async-start(bf16[8,3,16,2560]{3,2,1,0:T(8,128)(2,1)} %broadcast_in_dim.9), calls=%async_computation.2 | async-start | bytes 3932160 | tf_op jit(solution)/shard_map/all_to_all | solution.py:176
  73.1 13.2 %collective-permute-start.7 = (bf16[16,16,2560]{2,1,0:T(8,128)(2,1)}, bf16[16,16,2560]{2,1,0:T(8,128)(2,1)S(1)}, u32[]{:S(2)}, u32[]{:S(2)}) collective-permute-start(bf16[16,16,2560]{2,1,0:T(8,128)(2,1)} %all-to-all-done.cot_ref.one_ref), channel_id=1, source_target_pairs={{0,1},{1,0},{2,3},{3,2},{4,5},{5,4},{6,7},{7,6},{8,9},{9,8},{10,11... | collective-permute-start | bytes 3932168 | tf_op jit(solution)/shard_map/ppermute | solution.py:230
  86.3 5.5 %collective-permute-start.8 = (bf16[1,2,128,256]{3,2,1,0:T(8,128)(2,1)S(1)}, bf16[1,2,128,256]{3,2,1,0:T(8,128)(2,1)S(1)}, u32[]{:S(2)}, u32[]{:S(2)}) collective-permute-start(bf16[1,2,128,256]{3,2,1,0:T(8,128)(2,1)S(1)} %slice_bitcast_fusion), channel_id=1, source_target_pairs={{0,496},{16,480},{32,464},{48,448},{64,432},{80,416},{96,400},{112... | collective-permute-start | bytes 393224 | tf_op jit(solution)/shard_map/ppermute | solution.py:212
  91.8 9.9 %collective-permute-done.8.pre_far = bf16[1,2,128,256]{3,2,1,0:T(8,128)(2,1)S(1)} collective-permute-done((bf16[1,2,128,256]{3,2,1,0:T(8,128)(2,1)S(1)}, bf16[1,2,128,256]{3,2,1,0:T(8,128)(2,1)S(1)}, u32[]{:S(2)}, u32[]{:S(2)}) %collective-permute-start.8) | collective-permute-done | bytes 131104 | tf_op jit(solution)/shard_map/ppermute | solution.py:212
  101.7 0.0 collective-permute-done.7.one_came
  101.7 0.0 copy-start.2
  101.7 1.1 copy-done.2
  102.8 0.0 all-to-all-done.2.cot_ref.two_ref
  102.8 4.3 %shard_map.69 = bf16[8,16,2560]{2,1,0:T(8,128)(2,1)} custom-call(s32[2]{0:T(128)S(1)} %pad_add_fusion.where_ref, bf16[8,3,16,2560]{3,2,1,0:T(8,128)(2,1)S(1)} %all-to-all-done.2.cot_ref.two_ref, bf16[2,2560,256]{2,1,0:T(8,128)(2,1)} %bitcast.47, bf16[1,1280,256]{2,1,0:T(8,128)(2,1)} %collective-permute-done.refs_0_, ...), custom_call_target="tpu_custom_call" | custom-call | flops 671088640 | bytes 6553600 | tf_op jit(solution)/shard_map/pallas_call | solution.py:69
  107.0 1.9 %collective-permute-start.9 = (bf16[8,3,16,2560]{3,2,1,0:T(8,128)(2,1)S(1)}, bf16[8,3,16,2560]{3,2,1,0:T(8,128)(2,1)}, u32[]{:S(2)}, u32[]{:S(2)}) collective-permute-start(bf16[8,3,16,2560]{3,2,1,0:T(8,128)(2,1)S(1)} %all-to-all-done.2.cot_ref.two_ref), channel_id=1, source_target_pairs={{0,1},{1,0},{2,3},{3,2},{4,5},{5,4},{6,7},{7,6},{8,9},{9,8},{10,11... | collective-permute-start | bytes 5898248 | tf_op jit(solution)/shard_map/ppermute | solution.py:236
  109.0 6.9 %all-to-all-start.3 = ((bf16[16,8,2560]{2,1,0:T(8,128)(2,1)}), bf16[16,8,2560]{2,1,0:T(8,128)(2,1)S(1)}, u32[]{:S(2)}, u32[]{:S(2)}) async-start(bf16[16,8,2560]{2,1,0:T(8,128)(2,1)} %bitcast.55), calls=%async_computation.3 | async-start | bytes 1310720 | tf_op jit(solution)/shard_map/all_to_all | solution.py:235
  115.8 0.0 collective-permute-done.9.two_came
  115.8 0.0 copy-start.3
  115.9 1.3 %copy-done.3 = bf16[16,16,2560]{2,1,0:T(8,128)(2,1)S(1)} copy-done((bf16[16,16,2560]{2,1,0:T(8,128)(2,1)S(1)}, bf16[16,16,2560]{2,1,0:T(8,128)(2,1)}, u32[]{:S(2)}) %copy-start.3) | copy-done | bytes 1310744
  117.2 6.9 %shard_map.70 = bf16[2560,256]{1,0:T(8,128)(2,1)} custom-call(s32[2]{0:T(128)S(1)} %pad_add_fusion.where_ref, bf16[16,16,2560]{2,1,0:T(8,128)(2,1)} %all-to-all-done.cot_ref.one_ref, bf16[16,16,2560]{2,1,0:T(8,128)(2,1)S(1)} %copy-done.3, bf16[8,3,16,2560]{3,2,1,0:T(8,128)(2,1)S(1)} %all-to-all-done.2.cot_ref.two_ref, ...), custom_call_target="tpu_custom_call" | custom-call | flops 2013265920 | bytes 10485760 | tf_op jit(solution)/shard_map/pallas_call | solution.py:134
  124.0 5.6 %all-to-all-done.3 = bf16[16,8,2560]{2,1,0:T(8,128)(2,1)S(1)} async-done(((bf16[16,8,2560]{2,1,0:T(8,128)(2,1)}), bf16[16,8,2560]{2,1,0:T(8,128)(2,1)S(1)}, u32[]{:S(2)}, u32[]{:S(2)}) %all-to-all-start.3) | async-done | bytes 655392 | tf_op jit(solution)/shard_map/all_to_all | solution.py:235
  129.6 0.7 reduce_sum.25
  (8 shorter events, 0.1 us)
Async XLA Ops:
  2.9 8.4 %copy-start.1 = (bf16[1,2,2,128,256]{4,3,2,1,0:T(8,128)(2,1)S(1)}, bf16[1,2,2,128,256]{4,3,2,1,0:T(8,128)(2,1)}, u32[]{:S(2)}) copy-start(bf16[1,2,2,128,256]{4,3,2,1,0:T(8,128)(2,1)} %param.7) | copy-start | bytes 786436
  2.9 11.4 %copy-start = (bf16[1,2,2560,256]{3,2,1,0:T(8,128)(2,1)S(1)}, bf16[1,2,2560,256]{3,2,1,0:T(8,128)(2,1)}, u32[]{:S(2)}) copy-start(bf16[1,2,2560,256]{3,2,1,0:T(8,128)(2,1)} %param.5) | copy-start | bytes 7864324
  4.1 30.8 %all-to-all-start = ((bf16[16,16,2560]{2,1,0:T(8,128)(2,1)}), bf16[16,16,2560]{2,1,0:T(8,128)(2,1)}, u32[]{:S(2)}, u32[]{:S(2)}) async-start(bf16[16,16,2560]{2,1,0:T(8,128)(2,1)} %bitcast.53), calls=%async_computation | async-start | bytes 2621440 | tf_op jit(solution)/shard_map/all_to_all | solution.py:195
  12.0 22.9 %collective-permute-start.2 = (bf16[1,2,128,256]{3,2,1,0:T(8,128)(2,1)}, bf16[1,2,128,256]{3,2,1,0:T(8,128)(2,1)}, u32[]{:S(2)}, u32[]{:S(2)}) collective-permute-start(bf16[1,2,128,256]{3,2,1,0:T(8,128)(2,1)} %bitcast_select_fusion), channel_id=1, source_target_pairs={{0,1},{1,0},{2,3},{3,2},{4,5},{5,4},{6,7},{7,6},{8,9},{9,8},{10,11... | collective-permute-start | bytes 393224 | tf_op jit(solution)/shard_map/ppermute | solution.py:206
  15.5 19.4 %collective-permute-start.1 = (bf16[1,1280,256]{2,1,0:T(8,128)(2,1)}, bf16[1,1280,256]{2,1,0:T(8,128)(2,1)S(1)}, u32[]{:S(2)}, u32[]{:S(2)}) collective-permute-start(bf16[1,1280,256]{2,1,0:T(8,128)(2,1)} %get-tuple-element.20), channel_id=1, source_target_pairs={{0,1},{1,0},{2,3},{3,2},{4,5},{5,4},{6,7},{7,6},{8,9},{9,8},{10,11... | collective-permute-start | bytes 1966088 | tf_op jit(solution)/shard_map/ppermute | solution.py:201
  17.5 17.4 %collective-permute-start = (bf16[1,1280,256]{2,1,0:T(8,128)(2,1)}, bf16[1,1280,256]{2,1,0:T(8,128)(2,1)}, u32[]{:S(2)}, u32[]{:S(2)}) collective-permute-start(bf16[1,1280,256]{2,1,0:T(8,128)(2,1)} %get-tuple-element.21), channel_id=1, source_target_pairs={{0,1},{1,0},{2,3},{3,2},{4,5},{5,4},{6,7},{7,6},{8,9},{9,8},{10,11... | collective-permute-start | bytes 1966088 | tf_op jit(solution)/shard_map/ppermute | solution.py:201
  21.4 26.4 %collective-permute-start.3 = (bf16[2,8,2560]{2,1,0:T(8,128)(2,1)}, bf16[2,8,2560]{2,1,0:T(8,128)(2,1)}, u32[]{:S(2)}, u32[]{:S(2)}) collective-permute-start(bf16[2,8,2560]{2,1,0:T(8,128)(2,1)} %get-tuple-element.22), channel_id=1, source_target_pairs={{0,496},{16,480},{32,464},{48,448},{64,432},{80,416},{96,400},{112... | collective-permute-start | bytes 245768 | tf_op jit(solution)/shard_map/ppermute | solution.py:209
  32.9 14.9 %collective-permute-start.4 = (bf16[2,8,2560]{2,1,0:T(8,128)(2,1)}, bf16[2,8,2560]{2,1,0:T(8,128)(2,1)}, u32[]{:S(2)}, u32[]{:S(2)}) collective-permute-start(bf16[2,8,2560]{2,1,0:T(8,128)(2,1)} %get-tuple-element.23), channel_id=1, source_target_pairs={{0,497},{16,481},{32,465},{48,449},{64,433},{80,417},{96,401},{112... | collective-permute-start | bytes 245768 | tf_op jit(solution)/shard_map/ppermute | solution.py:210
  39.5 20.7 %all-to-all-start.1 = ((bf16[8,16,2560]{2,1,0:T(8,128)(2,1)}), bf16[8,16,2560]{2,1,0:T(8,128)(2,1)S(1)}, u32[]{:S(2)}, u32[]{:S(2)}) async-start(bf16[8,16,2560]{2,1,0:T(8,128)(2,1)} %shard_map.68), calls=%async_computation.1 | async-start | bytes 1310720 | tf_op jit(solution)/shard_map/all_to_all | solution.py:176
  60.4 7.5 %collective-permute-start.5 = (bf16[16,2560]{1,0:T(8,128)(2,1)S(1)}, bf16[16,2560]{1,0:T(8,128)(2,1)S(1)}, u32[]{:S(2)}, u32[]{:S(2)}) collective-permute-start(bf16[16,2560]{1,0:T(8,128)(2,1)S(1)} %get-tuple-element.26), channel_id=1, source_target_pairs={{16,0},{32,16},{48,32},{64,48},{80,64},{96,80},{112,96},{128,112},... | collective-permute-start | bytes 245768 | tf_op jit(solution)/shard_map/ppermute | solution.py:226
  62.4 5.5 %collective-permute-start.6 = (bf16[16,2560]{1,0:T(8,128)(2,1)S(1)}, bf16[16,2560]{1,0:T(8,128)(2,1)S(1)}, u32[]{:S(2)}, u32[]{:S(2)}) collective-permute-start(bf16[16,2560]{1,0:T(8,128)(2,1)S(1)} %get-tuple-element.27), channel_id=1, source_target_pairs={{1,481},{17,465},{33,449},{49,433},{65,417},{81,401},{97,385},{113... | collective-permute-start | bytes 245768 | tf_op jit(solution)/shard_map/ppermute | solution.py:225
  69.5 33.2 %all-to-all-start.2 = ((bf16[8,3,16,2560]{3,2,1,0:T(8,128)(2,1)}), bf16[8,3,16,2560]{3,2,1,0:T(8,128)(2,1)S(1)}, u32[]{:S(2)}, u32[]{:S(2)}) async-start(bf16[8,3,16,2560]{3,2,1,0:T(8,128)(2,1)} %broadcast_in_dim.9), calls=%async_computation.2 | async-start | bytes 3932160 | tf_op jit(solution)/shard_map/all_to_all | solution.py:176
  73.1 28.6 %collective-permute-start.7 = (bf16[16,16,2560]{2,1,0:T(8,128)(2,1)}, bf16[16,16,2560]{2,1,0:T(8,128)(2,1)S(1)}, u32[]{:S(2)}, u32[]{:S(2)}) collective-permute-start(bf16[16,16,2560]{2,1,0:T(8,128)(2,1)} %all-to-all-done.cot_ref.one_ref), channel_id=1, source_target_pairs={{0,1},{1,0},{2,3},{3,2},{4,5},{5,4},{6,7},{7,6},{8,9},{9,8},{10,11... | collective-permute-start | bytes 3932168 | tf_op jit(solution)/shard_map/ppermute | solution.py:230
  86.3 15.4 %collective-permute-start.8 = (bf16[1,2,128,256]{3,2,1,0:T(8,128)(2,1)S(1)}, bf16[1,2,128,256]{3,2,1,0:T(8,128)(2,1)S(1)}, u32[]{:S(2)}, u32[]{:S(2)}) collective-permute-start(bf16[1,2,128,256]{3,2,1,0:T(8,128)(2,1)S(1)} %slice_bitcast_fusion), channel_id=1, source_target_pairs={{0,496},{16,480},{32,464},{48,448},{64,432},{80,416},{96,400},{112... | collective-permute-start | bytes 393224 | tf_op jit(solution)/shard_map/ppermute | solution.py:212
  101.7 1.1 copy-start.2
  107.0 8.8 %collective-permute-start.9 = (bf16[8,3,16,2560]{3,2,1,0:T(8,128)(2,1)S(1)}, bf16[8,3,16,2560]{3,2,1,0:T(8,128)(2,1)}, u32[]{:S(2)}, u32[]{:S(2)}) collective-permute-start(bf16[8,3,16,2560]{3,2,1,0:T(8,128)(2,1)S(1)} %all-to-all-done.2.cot_ref.two_ref), channel_id=1, source_target_pairs={{0,1},{1,0},{2,3},{3,2},{4,5},{5,4},{6,7},{7,6},{8,9},{9,8},{10,11... | collective-permute-start | bytes 5898248 | tf_op jit(solution)/shard_map/ppermute | solution.py:236
  109.0 20.6 %all-to-all-start.3 = ((bf16[16,8,2560]{2,1,0:T(8,128)(2,1)}), bf16[16,8,2560]{2,1,0:T(8,128)(2,1)S(1)}, u32[]{:S(2)}, u32[]{:S(2)}) async-start(bf16[16,8,2560]{2,1,0:T(8,128)(2,1)} %bitcast.55), calls=%async_computation.3 | async-start | bytes 1310720 | tf_op jit(solution)/shard_map/all_to_all | solution.py:235
  115.8 1.3 %copy-start.3 = (bf16[16,16,2560]{2,1,0:T(8,128)(2,1)S(1)}, bf16[16,16,2560]{2,1,0:T(8,128)(2,1)}, u32[]{:S(2)}) copy-start(bf16[16,16,2560]{2,1,0:T(8,128)(2,1)} %copy-done.2) | copy-start | bytes 3932164
